TPU v7x, 512 devices: a whole 4x4x16 slice. The times are simulated.
512 devices in a mesh: atom: 32 (over z, core), kvec: 16 (over x, y).
Axes of the slice: x: 4, y: 4, z: 16, core: 2. Of those that a mesh axis runs over, the one named last changes fastest.
Arguments:
- features: float32 [49152, 256], P(('atom', 'kvec')), may hold values from -6 to 6
- fractions: int32 [3, 49152], P(None, 'atom'), may hold values from 0 to 1023
- wave_index: int32 [3, 8192], P(None, 'kvec'), may hold values from -12 to 12
- brick_count: int32 [32], replicated, may hold values from 1 to 1536, 24576 in all
- value_weight: float32 [256, 256], replicated, may hold values from -0.375 to 0.375
- k_filter: float32 [2, 8192, 256], P(None, 'kvec'), may hold values from -6 to 6
- mix_weight: float32 [2, 256, 256], replicated, may hold values from -0.25 to 0.25
- out_weight: float32 [256, 256], replicated, may hold values from -0.375 to 0.375
- norm_gain: float32 [256], replicated, may hold values from 0.5 to 1.5
- up_weight: float32 [256, 512], replicated, may hold values from -0.375 to 0.375
- down_weight: float32 [512, 256], replicated, may hold values from -0.25 to 0.25
Outputs:
- updated: float32 [49152, 256], P(('atom', 'kvec'))
Inputs may be any that keep to these rules, and one draw needn't show every extreme that they name: Brick b holds its atoms in its first brick_count[b] slots; the counts sum to 24576 and the largest equals 1536.
All inputs are finite; a program needn't handle non-finite values.
Results may differ from a plain program's by a relative error of at most 0.0003.
Values sent between devices are 32-bit elements; how exact they have to be, the bound alone decides.
No kernel may reach another device: no remote copies, remote signals or barrier semaphores. Data moves between devices by JAX's collectives and lax.ppermute only.
A program may use at most 64 MiB of HBM per device.

v0:
```python
import math

import jax
import jax.numpy as jnp
from jax import lax
from jax.sharding import PartitionSpec as P

phase_step = 2.0 * math.pi / 1024.0
exact = lax.Precision.HIGHEST


def laid_out(parts, dim):
    shape = list(parts.shape[1:])
    shape[dim] *= parts.shape[0]
    return jnp.moveaxis(parts, 0, dim).reshape(shape)


def copy_for_each(value, axis):
    peers = lax.axis_size(axis)
    return lax.all_to_all(
        jnp.broadcast_to(value[None], (peers, *value.shape)), axis, 0, 0, tiled=True
    )


def gather_directly(value, axis, dim):
    return laid_out(copy_for_each(value, axis), dim)


def cut_along(value, dim, peers):
    before, after = (value.shape[:dim], value.shape[dim + 1 :])
    return jnp.moveaxis(value.reshape(*before, peers, -1, *after), dim, 0)


def summed_on_arrival(value, axis, dim):
    peers = lax.axis_size(axis)
    parts = lax.all_to_all(cut_along(value, dim, peers), axis, 0, 0, tiled=True)
    return jnp.sum(parts, axis=0)


def sent_together(arrays, axis, dim, along):
    widths = [a.shape[along] for a in arrays]
    both = jnp.concatenate(arrays, axis=along)
    filled = summed_on_arrival(both, axis, dim)
    return tuple(jnp.split(filled, [sum(widths[:k]) for k in range(1, len(widths))], axis=along))


def sent_together_2(arrays, axis, dim, along):
    widths = [a.shape[along] for a in arrays]
    both = jnp.concatenate(arrays, axis=along)
    filled = lax.all_gather(both, axis, axis=dim, tiled=True)
    return tuple(jnp.split(filled, [sum(widths[:k]) for k in range(1, len(widths))], axis=along))


def phases(frac_rows, wave_index):
    phase_index = frac_rows[0][:, None] * wave_index[0][None, :]
    phase_index = phase_index + frac_rows[1][:, None] * wave_index[1][None, :]
    phase_index = phase_index + frac_rows[2][:, None] * wave_index[2][None, :]
    angles = jnp.mod(phase_index, 1024).astype(jnp.float32) * phase_step
    return (jnp.cos(angles), jnp.sin(angles))


def mixing(real_part, imag_part, filt_real, filt_imag, mix_weight, normalizer):
    mixed_real = real_part * filt_real - imag_part * filt_imag
    mixed_imag = real_part * filt_imag + imag_part * filt_real
    out_real = (
        jnp.dot(mixed_real, mix_weight[0], precision=exact)
        - jnp.dot(mixed_imag, mix_weight[1], precision=exact)
    ) * normalizer
    out_imag = (
        jnp.dot(mixed_real, mix_weight[1], precision=exact)
        + jnp.dot(mixed_imag, mix_weight[0], precision=exact)
    ) * normalizer
    return (out_real, out_imag)


def shards(
    features,
    fractions,
    wave_index,
    brick_count,
    value_weight,
    k_filter,
    mix_weight,
    out_weight,
    norm_gain,
    up_weight,
    down_weight,
):
    share_rows = features.shape[0]
    feat_width = features.shape[1]
    groups = lax.axis_size("kvec")
    bricks = lax.axis_size("atom")
    capacity = share_rows * groups
    k_shard = wave_index.shape[1]
    normalizer = 1.0 / math.sqrt(bricks * capacity // 2 * (k_shard * groups))
    own_brick = lax.axis_index("atom")
    own_group = lax.axis_index("kvec")
    brick_ids = jnp.arange(bricks, dtype=jnp.int32)
    brick_live = jnp.sum(jnp.where(brick_ids == own_brick, brick_count, 0))
    row_offset = own_group * share_rows
    local_slots = row_offset + jnp.arange(share_rows, dtype=jnp.int32)
    live_mask = (local_slots < brick_live).astype(jnp.float32)
    projected = jnp.dot(features, value_weight, precision=exact) * live_mask[:, None]
    contract = (((0,), (0,)), ((), ()))
    values = gather_directly(projected, "kvec", 0)
    block_rows = math.gcd(capacity, 512)

    def accumulate(counter, partial_value):
        begin = counter * block_rows
        value_rows = lax.dynamic_slice_in_dim(values, begin, block_rows, 0)
        cosine, sine_part = phases(
            lax.dynamic_slice_in_dim(fractions, begin, block_rows, 1), wave_index
        )
        real_part = partial_value[0] + lax.dot_general(
            cosine, value_rows, contract, precision=exact
        )
        imag_part = partial_value[1] - lax.dot_general(
            sine_part, value_rows, contract, precision=exact
        )
        return (real_part, imag_part)

    block_count = (brick_live + block_rows - 1) // block_rows
    empty_sums = jnp.zeros((k_shard, feat_width), jnp.float32)
    real_sf, imag_sf = lax.fori_loop(0, block_count, accumulate, (empty_sums, empty_sums))
    real_sf, imag_sf = sent_together((real_sf, imag_sf), "atom", 0, 1)
    share_k = real_sf.shape[0]
    offset = own_brick * share_k
    filt_re = lax.dynamic_slice_in_dim(k_filter[0], offset, share_k, 0)
    filt_im = lax.dynamic_slice_in_dim(k_filter[1], offset, share_k, 0)
    filt_real, filt_imag = mixing(real_sf, imag_sf, filt_re, filt_im, mix_weight, normalizer)
    filt_real, filt_imag = sent_together_2((filt_real, filt_imag), "atom", 0, 1)
    step_rows = math.gcd(share_rows * lax.axis_size("kvec"), 512)

    def one_block(counter, buffer):
        begin = counter * step_rows

        def compute(ignored):
            cosine, sine_part = phases(
                lax.dynamic_slice_in_dim(fractions, begin, step_rows, 1), wave_index
            )
            return jnp.dot(cosine, filt_real, precision=exact) - jnp.dot(
                sine_part, filt_imag, precision=exact
            )

        def nothing(ignored):
            return jnp.zeros((step_rows, feat_width), jnp.float32)

        part_rows = lax.cond(begin < brick_live, compute, nothing, 0)
        return lax.dynamic_update_slice_in_dim(buffer, part_rows, counter * step_rows, 0)

    messages = summed_on_arrival(
        lax.fori_loop(
            0,
            share_rows * lax.axis_size("kvec") // step_rows,
            one_block,
            jnp.zeros((share_rows * lax.axis_size("kvec"), feat_width), jnp.float32),
        ),
        "kvec",
        0,
    )
    residual = features + jnp.dot(messages, out_weight, precision=exact)
    normed = (
        residual
        * lax.rsqrt(jnp.mean(residual * residual, axis=1, keepdims=True) + 1e-06)
        * norm_gain
    )
    hidden = jax.nn.silu(jnp.dot(normed, up_weight, precision=exact))
    return (residual + jnp.dot(hidden, down_weight, precision=exact)) * live_mask[:, None]


def solution(mesh):
    return jax.shard_map(
        shards,
        mesh=mesh,
        in_specs=(
            P(("atom", "kvec"), None),
            P(None, "atom"),
            P(None, "kvec"),
            P(),
            P(),
            P(None, "kvec", None),
            P(),
            P(),
            P(),
            P(),
            P(),
        ),
        out_specs=P(("atom", "kvec"), None),
        check_vma=False,
    )
```

profile of v0, /device:TPU:448, one launch (start us, length us, event | category | flops | bytes accessed | tf_op | source)
XLA Modules:
  0.0 281.6 jit_solution(11271194533654472078)
XLA Ops:
  6.5 0.0 copy-start
  6.5 1.4 fusion.59
  7.9 0.6 compare_convert_fusion
  8.5 1.3 convolution_multiply_fusion
  9.8 1.3 broadcast_in_dim.10
  11.1 0.0 copy-start.3
  11.1 0.0 copy-start.6
  11.1 7.2 %all-to-all-start = ((f32[16,96,256]{2,1,0:T(8,128)}), f32[16,96,256]{2,1,0:T(8,128)S(1)}, u32[]{:S(2)}, u32[]{:S(2)}) async-start(f32[16,96,256]{2,1,0:T(8,128)} %broadcast_in_dim.10), calls=%async_computation | async-start | bytes 3145728 | tf_op jit(solution)/shard_map/all_to_all | solution.py:20
  18.9 23.2 %all-to-all-done = f32[16,96,256]{2,1,0:T(8,128)S(1)} async-done(((f32[16,96,256]{2,1,0:T(8,128)}), f32[16,96,256]{2,1,0:T(8,128)S(1)}, u32[]{:S(2)}, u32[]{:S(2)}) %all-to-all-start) | async-done | bytes 1572896 | tf_op jit(solution)/shard_map/all_to_all | solution.py:20
  42.2 0.0 copy-done.3
  42.2 0.0 copy-done.6
  42.2 36.1 %while.27 = (s32[]{:T(128)}, f32[512,256]{1,0:T(8,128)S(1)}, f32[512,256]{1,0:T(8,128)S(1)}, s32[]{:T(128)}, s32[3,1536]{1,0:T(4,128)S(1)}, /*index=5*/s32[3,512...) while((s32[]{:T(128)}, f32[512,256]{1,0:T(8,128)S(1)}, ...), condition=%wide.region_2.3_spmd, body=%wide.region_1.2_spmd.sunk | while | flops 1620312064 | bytes 3195095 | solution.py:124
  42.2 0.1 constant_dynamic-slice_fusion.3
  42.3 5.9 %convolution_subtract_fusion.4 = f32[512,256]{1,0:T(8,128)S(1)} fusion(f32[512,256]{1,0:T(8,128)S(1)} %get-tuple-element.416, s32[512]{0:T(512)S(1)} %bitcast.73, s32[512]{0:T(512)S(1)} %bitcast.69, s32[512]{0:T(512)S(1)} %bitcast.71, s32[512]{0:T(512)S(1)} %bitcast.67, s32[512]{0:T(512)S(1)} %bitcast.75, s32[512]{0:T(512)S(1)} %bitcast.65, ...), kind=kOutput, calls=%fused_computation.3.clone.1 | convolution fusion | flops 810156032 | bytes 1585156 | tf_op jit(solution)/shard_map/while/body/dot_general | solution.py:117
  48.2 5.9 %convolution_add_fusion.5 = f32[512,256]{1,0:T(8,128)S(1)} fusion(f32[512,256]{1,0:T(8,128)S(1)} %get-tuple-element.415, s32[512]{0:T(512)S(1)} %bitcast.74, s32[512]{0:T(512)S(1)} %bitcast.70, s32[512]{0:T(512)S(1)} %bitcast.72, s32[512]{0:T(512)S(1)} %bitcast.68, s32[512]{0:T(512)S(1)} %bitcast.76, s32[512]{0:T(512)S(1)} %bitcast.66, ...), kind=kOutput, calls=%fused_computation.4.clone.1 | convolution fusion | flops 810156032 | bytes 1585156 | tf_op jit(solution)/shard_map/while/body/dot_general | solution.py:114
  54.2 0.1 constant_dynamic-slice_fusion.3
  54.3 5.9 %convolution_subtract_fusion.4 = f32[512,256]{1,0:T(8,128)S(1)} fusion(f32[512,256]{1,0:T(8,128)S(1)} %get-tuple-element.416, s32[512]{0:T(512)S(1)} %bitcast.73, s32[512]{0:T(512)S(1)} %bitcast.69, s32[512]{0:T(512)S(1)} %bitcast.71, s32[512]{0:T(512)S(1)} %bitcast.67, s32[512]{0:T(512)S(1)} %bitcast.75, s32[512]{0:T(512)S(1)} %bitcast.65, ...), kind=kOutput, calls=%fused_computation.3.clone.1 | convolution fusion | flops 810156032 | bytes 1585156 | tf_op jit(solution)/shard_map/while/body/dot_general | solution.py:117
  60.2 5.9 %convolution_add_fusion.5 = f32[512,256]{1,0:T(8,128)S(1)} fusion(f32[512,256]{1,0:T(8,128)S(1)} %get-tuple-element.415, s32[512]{0:T(512)S(1)} %bitcast.74, s32[512]{0:T(512)S(1)} %bitcast.70, s32[512]{0:T(512)S(1)} %bitcast.72, s32[512]{0:T(512)S(1)} %bitcast.68, s32[512]{0:T(512)S(1)} %bitcast.76, s32[512]{0:T(512)S(1)} %bitcast.66, ...), kind=kOutput, calls=%fused_computation.4.clone.1 | convolution fusion | flops 810156032 | bytes 1585156 | tf_op jit(solution)/shard_map/while/body/dot_general | solution.py:114
  66.2 0.1 constant_dynamic-slice_fusion.3
  66.2 5.9 %convolution_subtract_fusion.4 = f32[512,256]{1,0:T(8,128)S(1)} fusion(f32[512,256]{1,0:T(8,128)S(1)} %get-tuple-element.416, s32[512]{0:T(512)S(1)} %bitcast.73, s32[512]{0:T(512)S(1)} %bitcast.69, s32[512]{0:T(512)S(1)} %bitcast.71, s32[512]{0:T(512)S(1)} %bitcast.67, s32[512]{0:T(512)S(1)} %bitcast.75, s32[512]{0:T(512)S(1)} %bitcast.65, ...), kind=kOutput, calls=%fused_computation.3.clone.1 | convolution fusion | flops 810156032 | bytes 1585156 | tf_op jit(solution)/shard_map/while/body/dot_general | solution.py:117
  72.2 5.9 %convolution_add_fusion.5 = f32[512,256]{1,0:T(8,128)S(1)} fusion(f32[512,256]{1,0:T(8,128)S(1)} %get-tuple-element.415, s32[512]{0:T(512)S(1)} %bitcast.74, s32[512]{0:T(512)S(1)} %bitcast.70, s32[512]{0:T(512)S(1)} %bitcast.72, s32[512]{0:T(512)S(1)} %bitcast.68, s32[512]{0:T(512)S(1)} %bitcast.76, s32[512]{0:T(512)S(1)} %bitcast.66, ...), kind=kOutput, calls=%fused_computation.4.clone.1 | convolution fusion | flops 810156032 | bytes 1585156 | tf_op jit(solution)/shard_map/while/body/dot_general | solution.py:114
  78.3 1.1 pad_maximum_fusion
  79.4 0.0 copy-start.2
  79.4 5.8 %all-to-all-start.1 = ((f32[32,16,512]{2,1,0:T(8,128)}), f32[32,16,512]{2,1,0:T(8,128)S(1)}, u32[]{:S(2)}, u32[]{:S(2)}) async-start(f32[32,16,512]{2,1,0:T(8,128)} %bitcast.13), calls=%async_computation.1 | async-start | bytes 2097152 | tf_op jit(solution)/shard_map/all_to_all | solution.py:36
  85.2 0.0 all-gather.2.cloned.1.call-start
  85.3 0.0 copy-done.2
  85.3 0.0 copy-start.1
  85.3 1.1 fusion.64
  86.4 52.0 %all-to-all-done.1 = f32[32,16,512]{2,1,0:T(8,128)S(1)} async-done(((f32[32,16,512]{2,1,0:T(8,128)}), f32[32,16,512]{2,1,0:T(8,128)S(1)}, u32[]{:S(2)}, u32[]{:S(2)}) %all-to-all-start.1) | async-done | bytes 1048608 | tf_op jit(solution)/shard_map/all_to_all | solution.py:36
  138.4 0.1 reduce_sum.37
  138.4 0.7 fusion.58
  139.2 0.0 copy-done.1
  139.2 0.2 fusion.40
  139.4 0.2 fusion.36
  139.6 0.3 fusion.35
  139.9 0.2 fusion.34
  140.1 0.6 pad_maximum_fusion.1
  140.7 0.0 all-gather.2.cloned.1.call-update
  140.8 62.5 %all-gather.2.cloned.1.call-done = f32[512,512]{1,0:T(8,128)} async-done(((f32[16,512]{1,0:T(8,128)}), f32[512,512]{1,0:T(8,128)}) %all-gather.2.cloned.1.call-update) | async-done | bytes 1048592 | tf_op jit(solution)/shard_map/all_gather | solution.py:50
  203.2 2.1 fusion.63
  205.3 0.1 broadcast_in_dim.8
  205.4 35.9 %while.28 = (s32[]{:T(128)}, f32[1536,256]{1,0:T(8,128)S(1)}, s32[]{:T(128)}, s32[3,1536]{1,0:T(4,128)S(1)}, s32[3,512]{1,0:T(4,128)S(1)}, /*index=5*/f32[512,25...) while((s32[]{:T(128)}, f32[1536,256]{1,0:T(8,128)S(1)}, ...), condition=%wide.region_7.8_spmd, body=%wide.region_4.7_spmd.sunk | while | flops 1620180992 | bytes 3719459 | solution.py:152
  206.1 11.3 %conditional.2 = (f32[512,256]{1,0:T(8,128)S(1)}) conditional(s32[]{:T(128)} %convert_element_type.48, () %tuple.77, (s32[]{:T(128)}, s32[3,1536]{1,0:T(4,128)S(1)}, s32[3,512]{1,0:T(4,128)S(1)}, f32[512,256]{1,0:T(8,128)}, f32[512,256]{1,0:T(8,128)S(1)}) %tuple.78), branch_computations={%region_5.5_spmd, %region_6.6_spmd} | conditional | flops 1620180992 | bytes 2670670 | solution.py:148
  206.1 0.1 constant_dynamic-slice_fusion.1
  206.2 6.1 %fusion.21 = f32[512,256]{1,0:T(8,128)S(1)} fusion(f32[512,256]{1,0:T(8,128)} %get-tuple-element.232, s32[512]{0:T(512)S(1)} %bitcast.85, s32[512]{0:T(512)S(1)} %bitcast.81, s32[512]{0:T(512)S(1)} %bitcast.83, s32[512]{0:T(512)S(1)} %bitcast.79, s32[512]{0:T(512)S(1)} %bitcast.87, s32[512]{0:T(512)S(1)} %bitcast.77), kind=kOutput, calls=%fused_computation.29 | convolution fusion | flops 810024960 | bytes 1060864 | tf_op jit(solution)/shard_map/while/body/eval_jaxpr/cond/branch_1_fun/dot_general | solution.py:141
  212.2 5.1 %convolution_subtract_fusion.1 = f32[512,256]{1,0:T(8,128)S(1)} fusion(f32[512,256]{1,0:T(8,128)S(1)} %fusion.21, f32[512,256]{1,0:T(8,128)S(1)} %get-tuple-element.233, s32[512]{0:T(512)S(1)} %bitcast.86, s32[512]{0:T(512)S(1)} %bitcast.82, s32[512]{0:T(512)S(1)} %bitcast.84, s32[512]{0:T(512)S(1)} %bitcast.80, s32[512]{0:T(512)S(1)} %bitcast.88, ...), kind=kOutput, calls=%fused_computation.24 | convolution fusion | flops 810156032 | bytes 1585152 | tf_op jit(solution)/shard_map/while/body/eval_jaxpr/cond/branch_1_fun/dot_general | solution.py:141
  218.0 11.3 %conditional.2 = (f32[512,256]{1,0:T(8,128)S(1)}) conditional(s32[]{:T(128)} %convert_element_type.48, () %tuple.77, (s32[]{:T(128)}, s32[3,1536]{1,0:T(4,128)S(1)}, s32[3,512]{1,0:T(4,128)S(1)}, f32[512,256]{1,0:T(8,128)}, f32[512,256]{1,0:T(8,128)S(1)}) %tuple.78), branch_computations={%region_5.5_spmd, %region_6.6_spmd} | conditional | flops 1620180992 | bytes 2670670 | solution.py:148
  218.0 0.1 constant_dynamic-slice_fusion.1
  218.1 6.1 %fusion.21 = f32[512,256]{1,0:T(8,128)S(1)} fusion(f32[512,256]{1,0:T(8,128)} %get-tuple-element.232, s32[512]{0:T(512)S(1)} %bitcast.85, s32[512]{0:T(512)S(1)} %bitcast.81, s32[512]{0:T(512)S(1)} %bitcast.83, s32[512]{0:T(512)S(1)} %bitcast.79, s32[512]{0:T(512)S(1)} %bitcast.87, s32[512]{0:T(512)S(1)} %bitcast.77), kind=kOutput, calls=%fused_computation.29 | convolution fusion | flops 810024960 | bytes 1060864 | tf_op jit(solution)/shard_map/while/body/eval_jaxpr/cond/branch_1_fun/dot_general | solution.py:141
  224.2 5.1 %convolution_subtract_fusion.1 = f32[512,256]{1,0:T(8,128)S(1)} fusion(f32[512,256]{1,0:T(8,128)S(1)} %fusion.21, f32[512,256]{1,0:T(8,128)S(1)} %get-tuple-element.233, s32[512]{0:T(512)S(1)} %bitcast.86, s32[512]{0:T(512)S(1)} %bitcast.82, s32[512]{0:T(512)S(1)} %bitcast.84, s32[512]{0:T(512)S(1)} %bitcast.80, s32[512]{0:T(512)S(1)} %bitcast.88, ...), kind=kOutput, calls=%fused_computation.24 | convolution fusion | flops 810156032 | bytes 1585152 | tf_op jit(solution)/shard_map/while/body/eval_jaxpr/cond/branch_1_fun/dot_general | solution.py:141
  230.0 11.3 %conditional.2 = (f32[512,256]{1,0:T(8,128)S(1)}) conditional(s32[]{:T(128)} %convert_element_type.48, () %tuple.77, (s32[]{:T(128)}, s32[3,1536]{1,0:T(4,128)S(1)}, s32[3,512]{1,0:T(4,128)S(1)}, f32[512,256]{1,0:T(8,128)}, f32[512,256]{1,0:T(8,128)S(1)}) %tuple.78), branch_computations={%region_5.5_spmd, %region_6.6_spmd} | conditional | flops 1620180992 | bytes 2670670 | solution.py:148
  230.0 0.1 constant_dynamic-slice_fusion.1
  230.1 6.1 %fusion.21 = f32[512,256]{1,0:T(8,128)S(1)} fusion(f32[512,256]{1,0:T(8,128)} %get-tuple-element.232, s32[512]{0:T(512)S(1)} %bitcast.85, s32[512]{0:T(512)S(1)} %bitcast.81, s32[512]{0:T(512)S(1)} %bitcast.83, s32[512]{0:T(512)S(1)} %bitcast.79, s32[512]{0:T(512)S(1)} %bitcast.87, s32[512]{0:T(512)S(1)} %bitcast.77), kind=kOutput, calls=%fused_computation.29 | convolution fusion | flops 810024960 | bytes 1060864 | tf_op jit(solution)/shard_map/while/body/eval_jaxpr/cond/branch_1_fun/dot_general | solution.py:141
  236.2 5.1 %convolution_subtract_fusion.1 = f32[512,256]{1,0:T(8,128)S(1)} fusion(f32[512,256]{1,0:T(8,128)S(1)} %fusion.21, f32[512,256]{1,0:T(8,128)S(1)} %get-tuple-element.233, s32[512]{0:T(512)S(1)} %bitcast.86, s32[512]{0:T(512)S(1)} %bitcast.82, s32[512]{0:T(512)S(1)} %bitcast.84, s32[512]{0:T(512)S(1)} %bitcast.80, s32[512]{0:T(512)S(1)} %bitcast.88, ...), kind=kOutput, calls=%fused_computation.24 | convolution fusion | flops 810156032 | bytes 1585152 | tf_op jit(solution)/shard_map/while/body/eval_jaxpr/cond/branch_1_fun/dot_general | solution.py:141
  241.3 29.8 %all_to_all.15 = f32[16,96,256]{2,1,0:T(8,128)} all-to-all(f32[16,96,256]{2,1,0:T(8,128)S(1)} %bitcast.63), channel_id=1, replica_groups=mesh['atom'=32,'kvec'=16] {'kvec'}, dimensions={0} | all-to-all | bytes 3145728 | tf_op jit(solution)/shard_map/all_to_all | solution.py:36
  271.2 1.6 reduce_sum.38
  272.7 0.0 copy-done.4
  272.8 0.0 copy-done.5
  272.8 0.4 multiply_reduce_fusion
  273.1 0.0 copy-done
  273.1 0.0 copy-done.7
  273.2 0.5 fusion.52
  273.6 0.0 copy-done.8
  273.6 1.1 fusion.33
  (10 shorter events, 0.2 us)
Async XLA Ops:
  6.5 266.6 %copy-start = (f32[256,512]{1,0:T(8,128)S(1)}, f32[256,512]{1,0:T(8,128)}, u32[]{:S(2)}) copy-start(f32[256,512]{1,0:T(8,128)} %param.26) | copy-start | bytes 1572868
  11.1 31.0 %copy-start.3 = (s32[3,512]{1,0:T(4,128)S(1)}, s32[3,512]{1,0:T(4,128)}, u32[]{:S(2)}) copy-start(s32[3,512]{1,0:T(4,128)} %param.19) | copy-start | bytes 18436
  11.1 31.0 %copy-start.6 = (s32[3,1536]{1,0:T(4,128)S(1)}, s32[3,1536]{1,0:T(4,128)}, u32[]{:S(2)}) copy-start(s32[3,1536]{1,0:T(4,128)} %param.18) | copy-start | bytes 55300
  11.1 31.0 %all-to-all-start = ((f32[16,96,256]{2,1,0:T(8,128)}), f32[16,96,256]{2,1,0:T(8,128)S(1)}, u32[]{:S(2)}, u32[]{:S(2)}) async-start(f32[16,96,256]{2,1,0:T(8,128)} %broadcast_in_dim.10), calls=%async_computation | async-start | bytes 3145728 | tf_op jit(solution)/shard_map/all_to_all | solution.py:20
  79.4 5.8 %copy-start.2 = (f32[2,512,256]{2,1,0:T(8,128)S(1)}, f32[2,512,256]{2,1,0:T(8,128)}, u32[]{:S(2)}) copy-start(f32[2,512,256]{2,1,0:T(8,128)} %param.22) | copy-start | bytes 3145732
  79.4 58.9 %all-to-all-start.1 = ((f32[32,16,512]{2,1,0:T(8,128)}), f32[32,16,512]{2,1,0:T(8,128)S(1)}, u32[]{:S(2)}, u32[]{:S(2)}) async-start(f32[32,16,512]{2,1,0:T(8,128)} %bitcast.13), calls=%async_computation.1 | async-start | bytes 2097152 | tf_op jit(solution)/shard_map/all_to_all | solution.py:36
  85.2 118.0 %all-gather.2.cloned.1.call-start = ((), (), s32[]{:S(2)}) async-start(), calls=%async_computation.3 | async-start | bytes 1081344 | tf_op jit(solution)/shard_map/all_gather | solution.py:50
  85.3 53.9 %copy-start.1 = (f32[2,256,256]{2,1,0:T(8,128)S(1)}, f32[2,256,256]{2,1,0:T(8,128)}, u32[]{:S(2)}) copy-start(f32[2,256,256]{2,1,0:T(8,128)} %param.23) | copy-start | bytes 1572868
  271.1 1.6 copy-start.4
  271.2 1.6 copy-start.5
  271.2 2.0 copy-start.7
  271.2 2.5 copy-start.8
Sparse Core Ops, SparseCore 0:
  140.9 62.2 all-gather.1
where the time goes:
time: 283 us; the launch traced here: 282 us
  waiting for transfers between devices  138 us (49%)
  matrix products  73.1 us (26%)
  blocking collectives  29.8 us (11%)
  between operations  14.2 us (5%)
  starting transfers between devices  13 us (5%)
  other arithmetic  6.16 us (2%)
  local copies, waits for them, and re-layouts  5.34 us (2%)
    all_gather x1, waiting for transfers between devices, sent_together_2(): filled = lax.all_gather(both, axis, axis=dim, tiled=True)  62.5 us
    all_to_all x1, waiting for transfers between devices, summed_on_arrival(): parts = lax.all_to_all(cut_along(value, dim, peers), axis, 0, 0, tiled=True)  52 us
    all_to_all x1, blocking collectives, summed_on_arrival(): parts = lax.all_to_all(cut_along(value, dim, peers), axis, 0, 0, tiled=True)  29.8 us
    all_to_all x1, waiting for transfers between devices, copy_for_each(): lax.all_to_all(jnp.broadcast_to(value[None], (peers, *value.shape)), axis...  23.2 us
    dot_general x3, matrix products, compute(): jnp.dot(cosine, filt_real, precision=exact)  18.2 us
    dot_general x3, matrix products, accumulate(): lax.dot_general(sine_part, value_rows, contract, precision=exact)  17.8 us
    dot_general x3, matrix products, accumulate(): lax.dot_general(cosine, value_rows, contract, precision=exact)  17.7 us
    dot_general x3, matrix products, compute(): jnp.dot(sine_part, filt_imag, precision=exact)  15.3 us
  transfers between devices with their start and end apart: 3, of which 3 were waited for; matrix products, arithmetic and copies ran while one was open for 0% of the time, Pallas kernels for 0%

commit v1 on v0

v1 whole, which is shorter than its diff:
```python
import math

import jax
import jax.numpy as jnp
from jax import lax
from jax.sharding import PartitionSpec as P

exact = lax.Precision.HIGHEST
high = lax.Precision.HIGH

SIN_HALF = (3.1415926401307073, -5.167710083507923, 2.5500775232148563, -0.5982912856211671, 0.07765766030589402)
COS_HALF = (0.9999999532476085, -4.934792830619664, 4.058411352862771, -1.3318765680813944, 0.21968961109803095)


def horner(x, coefficients):
    total = jnp.float32(coefficients[-1])
    for c in coefficients[-2::-1]:
        total = total * x + jnp.float32(c)
    return total


def cos_sin(turns):
    r = turns - jnp.round(turns)
    x = r * r
    s = r * horner(x, SIN_HALF)
    c = horner(x, COS_HALF)
    twice = s + s
    return 1.0 - twice * s, twice * c


def shards(
    features,
    fractions,
    wave_index,
    brick_count,
    value_weight,
    k_filter,
    mix_weight,
    out_weight,
    norm_gain,
    up_weight,
    down_weight,
):
    share = features.shape[0]
    width = features.shape[1]
    groups = lax.axis_size("kvec")
    bricks = lax.axis_size("atom")
    rings = bricks // 2
    capacity = share * groups
    k_shard = wave_index.shape[1]
    k_half = k_shard // 2
    k_own = k_half // rings
    normalizer = 1.0 / math.sqrt(bricks * capacity // 2 * (k_shard * groups))
    own_brick = lax.axis_index("atom")
    own_group = lax.axis_index("kvec")
    core = own_brick % 2
    along_z = own_brick // 2
    same_core = [[2 * z + c for z in range(rings)] for c in range(2)]
    swap = [(i, i ^ 1) for i in range(bricks)]
    brick_live = jnp.sum(jnp.where(jnp.arange(bricks, dtype=jnp.int32) == own_brick, brick_count, 0))

    gathered = lax.all_to_all(
        jnp.broadcast_to(features[None], (groups, share, width)), "kvec", 0, 0, tiled=True
    ).reshape(capacity, width)

    fracs = fractions.astype(jnp.float32)
    waves = wave_index.astype(jnp.float32) * (1.0 / 1024.0)
    waves_own = lax.dynamic_slice_in_dim(waves, core * k_half, k_half, 1)
    waves_other = lax.dynamic_slice_in_dim(waves, (1 - core) * k_half, k_half, 1)

    def turns(w):
        return (
            fracs[0][:, None] * w[0][None, :]
            + fracs[1][:, None] * w[1][None, :]
            + fracs[2][:, None] * w[2][None, :]
        )

    cos_own, sin_own = cos_sin(turns(waves_own))
    cos_other, sin_other = cos_sin(turns(waves_other))
    out_mix = jnp.stack(
        [jnp.dot(mix_weight[0], out_weight, precision=exact), jnp.dot(mix_weight[1], out_weight, precision=exact)]
    )

    live = (jnp.arange(capacity, dtype=jnp.int32) < brick_live)[:, None]
    values = jnp.where(live, gathered, 0.0)
    contract = (((0,), (0,)), ((), ()))

    def factors(cosine, sine):
        return jnp.concatenate(
            [
                lax.dot_general(cosine, values, contract, precision=high),
                -lax.dot_general(sine, values, contract, precision=high),
            ],
            axis=1,
        )

    passed = lax.ppermute(factors(cos_other, sin_other), "atom", swap)
    summed = factors(cos_own, sin_own) + passed
    parts = lax.all_to_all(
        summed.reshape(rings, k_own, 2 * width), "atom", 0, 0, axis_index_groups=same_core, tiled=True
    )
    total = jnp.sum(parts, axis=0)
    real_sf = jnp.dot(total[:, :width], value_weight, precision=exact)
    imag_sf = jnp.dot(total[:, width:], value_weight, precision=exact)
    offset = core * k_half + along_z * k_own
    filt = lax.dynamic_slice_in_dim(k_filter, offset, k_own, 1)
    u_re = real_sf * filt[0] - imag_sf * filt[1]
    u_im = real_sf * filt[1] + imag_sf * filt[0]
    t_re = (jnp.dot(u_re, out_mix[0], precision=exact) - jnp.dot(u_im, out_mix[1], precision=exact)) * normalizer
    t_im = (jnp.dot(u_re, out_mix[1], precision=exact) + jnp.dot(u_im, out_mix[0], precision=exact)) * normalizer
    mixed = jnp.concatenate([t_re, t_im], axis=1)
    t_own = lax.all_to_all(
        jnp.broadcast_to(mixed[None], (rings, k_own, 2 * width)),
        "atom",
        0,
        0,
        axis_index_groups=same_core,
        tiled=True,
    ).reshape(k_half, 2 * width)
    t_other = lax.ppermute(t_own, "atom", swap)

    def back(cosine, sine, t):
        return jnp.dot(cosine, t[:, :width], precision=high) - jnp.dot(sine, t[:, width:], precision=high)

    messages = back(cos_own, sin_own, t_own) + back(cos_other, sin_other, t_other)
    arrived = lax.all_to_all(messages.reshape(groups, share, width), "kvec", 0, 0, tiled=True)
    residual = features + jnp.sum(arrived, axis=0)
    normed = residual * lax.rsqrt(jnp.mean(residual * residual, axis=1, keepdims=True) + 1e-06) * norm_gain
    hidden = jax.nn.silu(jnp.dot(normed, up_weight, precision=exact))
    slots = own_group * share + jnp.arange(share, dtype=jnp.int32)
    keep = (slots < brick_live).astype(jnp.float32)[:, None]
    return (residual + jnp.dot(hidden, down_weight, precision=exact)) * keep


def solution(mesh):
    return jax.shard_map(
        shards,
        mesh=mesh,
        in_specs=(
            P(("atom", "kvec"), None),
            P(None, "atom"),
            P(None, "kvec"),
            P(),
            P(),
            P(None, "kvec", None),
            P(),
            P(),
            P(),
            P(),
            P(),
        ),
        out_specs=P(("atom", "kvec"), None),
        check_vma=False,
    )
```

time: 283 us -> 172 us (0.61)
  the two profiles are of different devices: /device:TPU:448 before, /device:TPU:1 now
where the time goes in v1:
time: 172 us; the launch traced here: 171 us
  waiting for transfers between devices  64.8 us (38%)
  starting transfers between devices  42.3 us (25%)
  blocking collectives  34 us (20%)
  matrix products  23.5 us (14%)
  local copies, waits for them, and re-layouts  3.48 us (2%)
  other arithmetic  2.62 us (2%)
    all_to_all x1, blocking collectives, shards(): lax.all_to_all(jnp.broadcast_to(mixed[None], (rings, k_own, 2 * width)),...  34 us
    all_to_all x1, waiting for transfers between devices, shards(): lax.all_to_all(summed.reshape(rings, k_own, 2 * width), 'atom', 0, 0, axi...  23.4 us
    all_to_all x1, waiting for transfers between devices, shards(): lax.all_to_all(messages.reshape(groups, share, width), 'kvec', 0, 0, tile...  23 us
    all_to_all x1, waiting for transfers between devices, shards(): lax.all_to_all(jnp.broadcast_to(features[None], (groups, share, width)),...  18.4 us
    all_to_all x1, starting transfers between devices, shards(): lax.all_to_all(summed.reshape(rings, k_own, 2 * width), 'atom', 0, 0, axi...  15.6 us
    ppermute x1, starting transfers between devices, shards(): t_other = lax.ppermute(t_own, 'atom', swap)  9.04 us
    all_to_all x1, starting transfers between devices, shards(): lax.all_to_all(jnp.broadcast_to(features[None], (groups, share, width)),...  7.72 us
    ppermute x1, starting transfers between devices, shards(): passed = lax.ppermute(factors(cos_other, sin_other), 'atom', swap)  6.22 us
  transfers between devices with their start and end apart: 5, of which 3 were waited for; matrix products, arithmetic and copies ran while one was open for 7% of the time, Pallas kernels for 0%

profile of v1, /device:TPU:1, one launch (start us, length us, event | category | flops | bytes accessed | tf_op | source)
XLA Modules:
  0.0 171.1 jit_solution(2779130993090588990)
XLA Ops:
  0.0 0.0 copy-start
  0.0 2.3 %broadcast_in_dim.34 = f32[16,96,256]{2,1,0:T(8,128)} broadcast(f32[96,256]{1,0:T(8,128)} %param.11), dimensions={1,2} | broadcast | bytes 1671168 | tf_op jit(solution)/shard_map/broadcast_in_dim | solution.py:63
  2.3 0.0 copy-start.5
  2.3 0.0 copy-start.9
  2.3 0.0 copy-start.6
  2.3 7.7 %all-to-all-start = ((f32[16,96,256]{2,1,0:T(8,128)}), f32[16,96,256]{2,1,0:T(8,128)S(1)}, u32[]{:S(2)}, u32[]{:S(2)}) async-start(f32[16,96,256]{2,1,0:T(8,128)} %broadcast_in_dim.34), calls=%async_computation | async-start | bytes 3145728 | tf_op jit(solution)/shard_map/all_to_all | solution.py:62
  10.0 0.0 copy-done.5
  10.1 0.0 copy-done.9
  10.1 0.6 fusion.47
  10.7 0.7 iota_compare_fusion
  11.4 0.0 copy-done.6
  11.4 0.1 constant_dynamic-slice_fusion
  11.5 0.1 slice_reduce_fusion.2
  11.5 18.4 %all-to-all-done = f32[16,96,256]{2,1,0:T(8,128)S(1)} async-done(((f32[16,96,256]{2,1,0:T(8,128)}), f32[16,96,256]{2,1,0:T(8,128)S(1)}, u32[]{:S(2)}, u32[]{:S(2)}) %all-to-all-start) | async-done | bytes 1572896 | tf_op jit(solution)/shard_map/all_to_all | solution.py:62
  29.9 0.3 bitcast_select_fusion
  30.2 2.4 %fusion.8 = f32[256,256]{0,1:T(8,128)S(1)} fusion(f32[1536,256]{1,0:T(8,128)S(1)} %bitcast_select_fusion, f32[256]{0:T(256)S(1)} %bitcast.59, f32[256]{0:T(256)S(1)} %bitcast.55, f32[256]{0:T(256)S(1)} %bitcast.51, f32[1536]{0:T(1024)S(1)} %get-tuple-element.6, f32[1536]{0:T(1024)S(1)} %get-tuple-element.7, f32[1536]{0:T(1024)S(1)} %get-tuple-element.5), kind=kOutput, calls=%fused_computation.22 | convolution fusion | flops 611844096 | bytes 1856512 | tf_op jit(solution)/shard_map/dot_general | solution.py:91
  32.5 2.7 %convolution_negate_fusion = f32[256,256]{0,1:T(8,128)S(1)} fusion(f32[1536,256]{1,0:T(8,128)S(1)} %bitcast_select_fusion, f32[256]{0:T(256)S(1)} %bitcast.60, f32[256]{0:T(256)S(1)} %bitcast.56, f32[256]{0:T(256)S(1)} %bitcast.52, f32[1536]{0:T(1024)S(1)} %get-tuple-element.6, f32[1536]{0:T(1024)S(1)} %get-tuple-element.7, f32[1536]{0:T(1024)S(1)} %get-tuple-element.5), kind=kOutput, calls=%fused_computation.25 | convolution fusion | flops 614662144 | bytes 1856512 | tf_op jit(solution)/shard_map/dot_general | solution.py:92
  35.2 6.2 %collective-permute-start = (f32[256,512]{0,1:T(8,128)S(1)}, f32[256,512]{0,1:T(8,128)S(1)}, u32[]{:S(2)}, u32[]{:S(2)}) collective-permute-start(f32[256,512]{0,1:T(8,128)S(1)} %pad_maximum_fusion), channel_id=1, source_target_pairs={{0,16},{16,0},{32,48},{48,32},{64,80},{80,64},{96,112},{112,96},{1... | collective-permute-start | bytes 1572872 | tf_op jit(solution)/shard_map/ppermute | solution.py:97
  41.5 2.4 %fusion.12 = f32[256,256]{0,1:T(8,128)S(1)} fusion(f32[1536,256]{1,0:T(8,128)S(1)} %bitcast_select_fusion, f32[256]{0:T(256)S(1)} %bitcast.71, f32[1536]{0:T(1024)S(1)} %get-tuple-element.6, f32[256]{0:T(256)S(1)} %bitcast.63, f32[1536]{0:T(1024)S(1)} %get-tuple-element.7, f32[256]{0:T(256)S(1)} %bitcast.67, f32[1536]{0:T(1024)S(1)} %get-tuple-element.5), kind=kOutput, calls=%fused_computation.24 | convolution fusion | flops 611844096 | bytes 1856512 | tf_op jit(solution)/shard_map/dot_general | solution.py:91
  43.9 2.7 %convolution_negate_fusion.1 = f32[256,256]{0,1:T(8,128)S(1)} fusion(f32[1536,256]{1,0:T(8,128)S(1)} %bitcast_select_fusion, f32[256]{0:T(256)S(1)} %bitcast.72, f32[1536]{0:T(1024)S(1)} %get-tuple-element.6, f32[256]{0:T(256)S(1)} %bitcast.64, f32[1536]{0:T(1024)S(1)} %get-tuple-element.7, f32[256]{0:T(256)S(1)} %bitcast.68, f32[1536]{0:T(1024)S(1)} %get-tuple-element.5), kind=kOutput, calls=%fused_computation.26 | convolution fusion | flops 614662144 | bytes 1856512 | tf_op jit(solution)/shard_map/dot_general | solution.py:92
  46.5 0.0 copy-start.1
  46.5 0.0 copy-start.3
  46.5 0.0 collective-permute-done
  46.5 0.1 maximum_add_fusion
  46.6 1.0 copy.12
  47.6 0.0 copy-start.2
  47.6 15.6 %all-to-all-start.1 = ((f32[16,16,512]{2,1,0:T(8,128)}), f32[16,16,512]{2,1,0:T(8,128)S(1)}, u32[]{:S(2)}, u32[]{:S(2)}) async-start(f32[16,16,512]{2,1,0:T(8,128)} %bitcast.7), calls=%async_computation.1 | async-start | bytes 1048576 | tf_op jit(solution)/shard_map/all_to_all | solution.py:99
  63.2 0.0 copy-done.1
  63.2 0.0 copy-done.3
  63.2 0.4 fusion.28
  63.6 0.4 fusion.26
  64.0 23.4 %all-to-all-done.1 = f32[16,16,512]{2,1,0:T(8,128)S(1)} async-done(((f32[16,16,512]{2,1,0:T(8,128)}), f32[16,16,512]{2,1,0:T(8,128)S(1)}, u32[]{:S(2)}, u32[]{:S(2)}) %all-to-all-start.1) | async-done | bytes 524320 | tf_op jit(solution)/shard_map/all_to_all | solution.py:99
  87.4 0.0 copy-done.2
  87.4 0.2 fusion.45
  87.6 1.0 multiply_add_fusion
  88.6 0.2 fusion.113
  88.8 0.2 fusion.114
  89.1 0.3 fusion.16
  89.3 0.2 fusion.15
  89.6 0.1 broadcast_in_dim.36
  89.6 34.0 %all_to_all.20 = f32[16,16,512]{2,1,0:T(8,128)S(1)} all-to-all(f32[16,16,512]{2,1,0:T(8,128)S(1)} %broadcast_in_dim.36), channel_id=1, replica_groups={{0,32,64,96,128,160,192,224,256,288,320,352,384,416,448,480},{16,48,80,..., dimensions={0} | all-to-all | bytes 1048576 | tf_op jit(solution)/shard_map/all_to_all | solution.py:112
  123.6 9.0 %collective-permute-start.1 = (f32[256,512]{1,0:T(8,128)S(1)}, f32[256,512]{1,0:T(8,128)S(1)}, u32[]{:S(2)}, u32[]{:S(2)}) collective-permute-start(f32[256,512]{1,0:T(8,128)S(1)} %bitcast.48), channel_id=1, source_target_pairs={{0,16},{16,0},{32,48},{48,32},{64,80},{80,64},{96,112},{112,96},{1... | collective-permute-start | bytes 1572872 | tf_op jit(solution)/shard_map/ppermute | solution.py:120
  132.7 1.8 %fusion.10 = f32[1536,256]{1,0:T(8,128)S(1)} fusion(f32[256]{0:T(256)S(1)} %bitcast.73, f32[1536]{0:T(1024)S(1)} %get-tuple-element.6, f32[256]{0:T(256)S(1)} %bitcast.65, f32[1536]{0:T(1024)S(1)} %get-tuple-element.7, f32[256]{0:T(256)S(1)} %bitcast.69, f32[1536]{0:T(1024)S(1)} %get-tuple-element.5, f32[256,512]{1,0:T(8,128)S(1)} %bitcast.49), kind=kOutput, calls=%fused_computation.23 | convolution fusion | flops 611844096 | bytes 1862656 | tf_op jit(solution)/shard_map/dot_general | solution.py:123
  134.5 2.1 %convolution_subtract_fusion.1 = f32[1536,256]{1,0:T(8,128)S(1)} fusion(f32[1536,256]{1,0:T(8,128)S(1)} %fusion.10, f32[256]{0:T(256)S(1)} %bitcast.74, f32[1536]{0:T(1024)S(1)} %get-tuple-element.6, f32[256]{0:T(256)S(1)} %bitcast.66, f32[1536]{0:T(1024)S(1)} %get-tuple-element.7, f32[256]{0:T(256)S(1)} %bitcast.70, f32[1536]{0:T(1024)S(1)} %get-tuple-element.5, ...), kind=kOutput, calls=%fused_computation.2 | convolution fusion | flops 614989824 | bytes 3435520 | tf_op jit(solution)/shard_map/dot_general | solution.py:123
  136.6 0.0 collective-permute-done.1
  136.6 2.1 %fusion.17 = f32[1536,256]{1,0:T(8,128)S(1)} fusion(f32[256]{0:T(256)S(1)} %bitcast.61, f32[256]{0:T(256)S(1)} %bitcast.57, f32[256]{0:T(256)S(1)} %bitcast.53, f32[1536]{0:T(1024)S(1)} %get-tuple-element.6, f32[1536]{0:T(1024)S(1)} %get-tuple-element.7, f32[1536]{0:T(1024)S(1)} %get-tuple-element.5, f32[256,512]{1,0:T(8,128)S(1)} %collective-permute-done.1), kind=kOutput, calls=%fused_computation.33 | convolution fusion | flops 614596608 | bytes 1862656 | tf_op jit(solution)/shard_map/dot_general | solution.py:123
  138.7 3.1 %fusion = f32[1536,256]{1,0:T(8,128)} fusion(f32[1536,256]{1,0:T(8,128)S(1)} %convolution_subtract_fusion.1, f32[1536,256]{1,0:T(8,128)S(1)} %fusion.17, f32[256]{0:T(256)S(1)} %bitcast.62, f32[256]{0:T(256)S(1)} %bitcast.58, f32[256]{0:T(256)S(1)} %bitcast.54, f32[1536]{0:T(1024)S(1)} %get-tuple-element.6, f32[1536]{0:T(1024)S(1)} %get-tuple-element.7, ...), kind=kOutput, calls=%fused_computation.1 | convolution fusion | flops 612630528 | bytes 5008384 | tf_op jit(solution)/shard_map/dot_general | solution.py:123
  141.8 3.7 %all-to-all-start.3 = ((f32[16,96,256]{2,1,0:T(8,128)}), f32[16,96,256]{2,1,0:T(8,128)S(1)}, u32[]{:S(2)}, u32[]{:S(2)}) async-start(f32[16,96,256]{2,1,0:T(8,128)} %bitcast.47), calls=%async_computation.3 | async-start | bytes 3145728 | tf_op jit(solution)/shard_map/all_to_all | solution.py:126
  145.5 0.0 copy-start.4
  145.5 0.0 copy-start.7
  145.6 0.0 copy-start.8
  145.6 0.7 compare_convert_fusion
  146.3 23.0 %all-to-all-done.3 = f32[16,96,256]{2,1,0:T(8,128)S(1)} async-done(((f32[16,96,256]{2,1,0:T(8,128)}), f32[16,96,256]{2,1,0:T(8,128)S(1)}, u32[]{:S(2)}, u32[]{:S(2)}) %all-to-all-start.3) | async-done | bytes 1572896 | tf_op jit(solution)/shard_map/all_to_all | solution.py:126
  169.3 0.1 reduce_sum.38
  169.4 0.0 copy-done.4
  169.4 0.1 multiply_reduce_fusion
  169.6 0.0 copy-done
  169.6 0.0 copy-done.7
  169.6 0.5 fusion.38
  170.1 0.0 copy-done.8
  170.1 1.1 fusion.14
  (6 shorter events, 0.1 us)
Async XLA Ops:
  0.0 169.6 %copy-start = (f32[256,512]{1,0:T(8,128)S(1)}, f32[256,512]{1,0:T(8,128)}, u32[]{:S(2)}) copy-start(f32[256,512]{1,0:T(8,128)} %param.20) | copy-start | bytes 1572868
  2.3 7.8 %copy-start.5 = (s32[3,1536]{1,0:T(4,128)S(1)}, s32[3,1536]{1,0:T(4,128)}, u32[]{:S(2)}) copy-start(s32[3,1536]{1,0:T(4,128)} %param.12) | copy-start | bytes 55300
  2.3 7.8 %copy-start.9 = (s32[32]{0:T(128)S(1)}, s32[32]{0:T(128)}, u32[]{:S(2)}) copy-start(s32[32]{0:T(128)} %param.14) | copy-start | bytes 388
  2.3 9.1 %copy-start.6 = (s32[3,512]{1,0:T(4,128)S(1)}, s32[3,512]{1,0:T(4,128)}, u32[]{:S(2)}) copy-start(s32[3,512]{1,0:T(4,128)} %param.13) | copy-start | bytes 18436
  2.3 27.6 %all-to-all-start = ((f32[16,96,256]{2,1,0:T(8,128)}), f32[16,96,256]{2,1,0:T(8,128)S(1)}, u32[]{:S(2)}, u32[]{:S(2)}) async-start(f32[16,96,256]{2,1,0:T(8,128)} %broadcast_in_dim.34), calls=%async_computation | async-start | bytes 3145728 | tf_op jit(solution)/shard_map/all_to_all | solution.py:62
  35.2 11.3 %collective-permute-start = (f32[256,512]{0,1:T(8,128)S(1)}, f32[256,512]{0,1:T(8,128)S(1)}, u32[]{:S(2)}, u32[]{:S(2)}) collective-permute-start(f32[256,512]{0,1:T(8,128)S(1)} %pad_maximum_fusion), channel_id=1, source_target_pairs={{0,16},{16,0},{32,48},{48,32},{64,80},{80,64},{96,112},{112,96},{1... | collective-permute-start | bytes 1572872 | tf_op jit(solution)/shard_map/ppermute | solution.py:97
  46.5 16.7 %copy-start.1 = (f32[256,256]{1,0:T(8,128)S(1)}, f32[256,256]{1,0:T(8,128)}, u32[]{:S(2)}) copy-start(f32[256,256]{1,0:T(8,128)} %param.18) | copy-start | bytes 786436
  46.5 16.7 %copy-start.3 = (f32[2,256,256]{2,1,0:T(8,128)S(1)}, f32[2,256,256]{2,1,0:T(8,128)}, u32[]{:S(2)}) copy-start(f32[2,256,256]{2,1,0:T(8,128)} %param.17) | copy-start | bytes 1572868
  47.6 39.8 %copy-start.2 = (f32[256,256]{1,0:T(8,128)S(1)}, f32[256,256]{1,0:T(8,128)}, u32[]{:S(2)}) copy-start(f32[256,256]{1,0:T(8,128)} %param.15) | copy-start | bytes 786436
  47.6 39.8 %all-to-all-start.1 = ((f32[16,16,512]{2,1,0:T(8,128)}), f32[16,16,512]{2,1,0:T(8,128)S(1)}, u32[]{:S(2)}, u32[]{:S(2)}) async-start(f32[16,16,512]{2,1,0:T(8,128)} %bitcast.7), calls=%async_computation.1 | async-start | bytes 1048576 | tf_op jit(solution)/shard_map/all_to_all | solution.py:99
  123.6 12.9 %collective-permute-start.1 = (f32[256,512]{1,0:T(8,128)S(1)}, f32[256,512]{1,0:T(8,128)S(1)}, u32[]{:S(2)}, u32[]{:S(2)}) collective-permute-start(f32[256,512]{1,0:T(8,128)S(1)} %bitcast.48), channel_id=1, source_target_pairs={{0,16},{16,0},{32,48},{48,32},{64,80},{80,64},{96,112},{112,96},{1... | collective-permute-start | bytes 1572872 | tf_op jit(solution)/shard_map/ppermute | solution.py:120
  141.8 27.5 %all-to-all-start.3 = ((f32[16,96,256]{2,1,0:T(8,128)}), f32[16,96,256]{2,1,0:T(8,128)S(1)}, u32[]{:S(2)}, u32[]{:S(2)}) async-start(f32[16,96,256]{2,1,0:T(8,128)} %bitcast.47), calls=%async_computation.3 | async-start | bytes 3145728 | tf_op jit(solution)/shard_map/all_to_all | solution.py:126
  145.5 23.9 %copy-start.4 = (f32[96,256]{1,0:T(8,128)S(1)}, f32[96,256]{1,0:T(8,128)}, u32[]{:S(2)}) copy-start(f32[96,256]{1,0:T(8,128)} %param.11) | copy-start | bytes 294916
  145.5 24.0 %copy-start.7 = (f32[256]{0:T(256)S(1)}, f32[256]{0:T(256)}, u32[]{:S(2)}) copy-start(f32[256]{0:T(256)} %param.19) | copy-start | bytes 3076
  145.6 24.5 %copy-start.8 = (f32[512,256]{1,0:T(8,128)S(1)}, f32[512,256]{1,0:T(8,128)}, u32[]{:S(2)}) copy-start(f32[512,256]{1,0:T(8,128)} %param.21) | copy-start | bytes 1572868

commit v2 on v1

v2 whole, which is shorter than its diff:
```python
import math

import jax
import jax.numpy as jnp
from jax import lax
from jax.sharding import Mesh
from jax.sharding import PartitionSpec as P

exact = lax.Precision.HIGHEST
high = lax.Precision.HIGH
NEAR = 4

SIN_HALF = (3.1415926401307073, -5.167710083507923, 2.5500775232148563, -0.5982912856211671, 0.07765766030589402)


def cos_turns(turns):
    r = turns - jnp.round(turns)
    x = r * r
    total = jnp.float32(SIN_HALF[-1])
    for c in SIN_HALF[-2::-1]:
        total = total * x + jnp.float32(c)
    s = r * total
    return 1.0 - (s + s) * s


def exchange(blocks, axes):
    return lax.all_to_all(blocks, axes, 0, 0, tiled=True)


def to_all(block, axes):
    peers = lax.axis_size(axes)
    return exchange(jnp.broadcast_to(block[None], (peers, *block.shape)), axes)


def swap_cores(block):
    return lax.ppermute(block, "core", [(0, 1), (1, 0)])


def shards(
    features,
    fractions,
    wave_index,
    brick_count,
    value_weight,
    k_filter,
    mix_weight,
    out_weight,
    norm_gain,
    up_weight,
    down_weight,
):
    share, width = features.shape
    groups = lax.axis_size("kvec")
    far, near = lax.axis_size("far"), lax.axis_size("near")
    rings = far * near
    capacity = share * groups
    k_shard = wave_index.shape[1]
    k_half = k_shard // 2
    k_own = k_half // rings
    rows = 2 * k_own
    normalizer = 1.0 / math.sqrt(rings * capacity * (k_shard * groups))
    core = lax.axis_index("core")
    own_group = lax.axis_index("kvec")
    own_brick = (lax.axis_index("far") * near + lax.axis_index("near")) * 2 + core
    count = lax.dynamic_index_in_dim(brick_count, own_brick, 0, False)

    values = to_all(features, "kvec").reshape(capacity, width)

    live = (jnp.arange(capacity, dtype=jnp.int32) < count).astype(jnp.float32)
    fracs = fractions.astype(jnp.float32)
    waves = wave_index.astype(jnp.float32) * (1.0 / 1024.0)
    quarter = jnp.broadcast_to(jnp.array([0.0, 0.25], jnp.float32)[None, :, None], (rings, 2, k_own)).reshape(-1)

    def lines(which):
        w = lax.dynamic_slice_in_dim(waves, which * k_half, k_half, 1).reshape(3, rings, 1, k_own)
        return jnp.broadcast_to(w, (3, rings, 2, k_own)).reshape(3, 2 * k_half)

    def basis(w):
        turns = sum(fracs[j][:, None] * w[j][None, :] for j in range(3)) + quarter[None, :]
        return cos_turns(turns) * live[:, None]

    def basis_t(w):
        turns = sum(w[j][:, None] * fracs[j][None, :] for j in range(3)) + quarter[:, None]
        return cos_turns(turns) * live[None, :]

    w_own, w_other = lines(core), lines(1 - core)
    own, other, own_t, other_t = lax.optimization_barrier(
        (basis(w_own), basis(w_other), basis_t(w_own), basis_t(w_other))
    )
    out_mix = jnp.stack(
        [jnp.dot(mix_weight[0], out_weight, precision=exact), jnp.dot(mix_weight[1], out_weight, precision=exact)]
    )

    passed = swap_cores(jnp.dot(other_t, values, precision=high))
    summed = lax.optimization_barrier(jnp.dot(own_t, values, precision=high)) + passed
    close = jnp.sum(exchange(summed.reshape(near, far * rows, width), "near"), axis=0)
    raw = jnp.sum(lax.all_gather(close, "far", axis=0), axis=0)
    total = jnp.dot(raw, value_weight, precision=exact).reshape(far, 2, k_own, width)
    real_sf, imag_sf = total[:, 0], total[:, 1]
    kept = far * k_own
    filt = lax.dynamic_slice_in_dim(k_filter, core * k_half + lax.axis_index("near") * kept, kept, 1) * normalizer
    filt = filt.reshape(2, far, k_own, width)
    u_re = real_sf * filt[0] - imag_sf * filt[1]
    u_im = real_sf * filt[1] + imag_sf * filt[0]
    mixed = jnp.dot(jnp.stack([u_re, u_im], axis=1).reshape(far * rows, width), out_mix[0], precision=exact) + jnp.dot(
        jnp.stack([-u_im, u_re], axis=1).reshape(far * rows, width), out_mix[1], precision=exact
    )

    t_own = to_all(mixed, "near").reshape(rings * rows, width)
    t_other = swap_cores(t_own)
    messages = jnp.dot(own, t_own, precision=high) + jnp.dot(other, t_other, precision=high)
    landed = exchange(messages.reshape(groups, share, width), "kvec")
    residual = features + jnp.sum(landed, axis=0)
    normed = residual * lax.rsqrt(jnp.mean(residual * residual, axis=1, keepdims=True) + 1e-06) * norm_gain
    hidden = jax.nn.silu(jnp.dot(normed, up_weight, precision=exact))
    slots = own_group * share + jnp.arange(share, dtype=jnp.int32)
    keep = (slots < count).astype(jnp.float32)[:, None]
    return (residual + jnp.dot(hidden, down_weight, precision=exact)) * keep


def solution(mesh):
    bricks, groups = mesh.shape["atom"], mesh.shape["kvec"]
    grid = Mesh(
        mesh.devices.reshape(bricks // 2 // NEAR, NEAR, 2, groups), ("far", "near", "core", "kvec")
    )
    atom = ("far", "near", "core")
    return jax.shard_map(
        shards,
        mesh=grid,
        in_specs=(
            P((*atom, "kvec"), None),
            P(None, atom),
            P(None, "kvec"),
            P(),
            P(),
            P(None, "kvec", None),
            P(),
            P(),
            P(),
            P(),
            P(),
        ),
        out_specs=P((*atom, "kvec"), None),
        check_vma=False,
    )
```

time: 172 us -> 148 us (0.86)
  waiting for transfers between devices: 64.8 us -> 37.6 us
  other arithmetic: 2.62 us -> 16.9 us
  starting transfers between devices: 42.3 us -> 28.1 us
  blocking collectives: 34 us -> 47.7 us
  matrix products: 23.5 us -> 12.1 us
    all_gather x0 -> x1, blocking collectives: none -> 31 us  [shards(): raw = jnp.sum(lax.all_gather(close, 'far', axis=0), axis=0)]
    all_to_all x3, waiting for transfers between devices: 64.8 us -> 37.5 us  [exchange(): return lax.all_to_all(blocks, axes, 0, 0, tiled=True)]
    all_to_all x1, blocking collectives: 34 us -> 16.7 us  [exchange(): return lax.all_to_all(blocks, axes, 0, 0, tiled=True)]
    mul x0 -> x3, other arithmetic: none -> 14.4 us  [the longest x1 6.82 us: basis_t(): return cos_turns(turns) * live[None, :]]
    dot_general x14 -> x7, matrix products: 21.2 us -> 9.8 us  [the longest x1 3.46 us: shards(): passed = swap_cores(jnp.dot(other_t, values, precision=high))]
    all_to_all x3, starting transfers between devices: 27 us -> 17.9 us  [exchange(): return lax.all_to_all(blocks, axes, 0, 0, tiled=True)]
    ppermute x2, starting transfers between devices: 15.3 us -> 10.2 us  [swap_cores(): return lax.ppermute(block, 'core', [(0, 1), (1, 0)])]
  transfers between devices with their start and end apart: 5 -> 5, of which waited for: 3 -> 3; matrix products, arithmetic and copies ran while one was open for 7% -> 14% of each run, Pallas kernels for 0% -> 0%
where the time goes in v2:
time: 148 us; the launch traced here: 147 us
  blocking collectives  47.7 us (32%)
  waiting for transfers between devices  37.6 us (25%)
  starting transfers between devices  28.1 us (19%)
  other arithmetic  16.9 us (11%)
  matrix products  12.1 us (8%)
  local copies, waits for them, and re-layouts  4.38 us (3%)
    all_to_all x3, waiting for transfers between devices, exchange(): return lax.all_to_all(blocks, axes, 0, 0, tiled=True)  37.5 us
    all_gather x1, blocking collectives, shards(): raw = jnp.sum(lax.all_gather(close, 'far', axis=0), axis=0)  31 us
    all_to_all x3, starting transfers between devices, exchange(): return lax.all_to_all(blocks, axes, 0, 0, tiled=True)  17.9 us
    all_to_all x1, blocking collectives, exchange(): return lax.all_to_all(blocks, axes, 0, 0, tiled=True)  16.7 us
    ppermute x2, starting transfers between devices, swap_cores(): return lax.ppermute(block, 'core', [(0, 1), (1, 0)])  10.2 us
    mul x1, other arithmetic, basis_t(): return cos_turns(turns) * live[None, :]  6.82 us
    mul x1, other arithmetic, basis(): return cos_turns(turns) * live[:, None]  6.63 us
    dot_general x1, matrix products, shards(): passed = swap_cores(jnp.dot(other_t, values, precision=high))  3.46 us
  transfers between devices with their start and end apart: 5, of which 3 were waited for; matrix products, arithmetic and copies ran while one was open for 14% of the time, Pallas kernels for 0%

profile of v2, /device:TPU:1, one launch (start us, length us, event | category | flops | bytes accessed | tf_op | source)
XLA Modules:
  0.0 147.1 jit_solution(16248081490518761486)
XLA Ops:
  0.0 0.0 copy-start
  0.0 0.0 copy-start.9
  0.0 0.0 copy-start.8
  0.0 2.3 %broadcast_in_dim.68 = f32[16,96,256]{2,1,0:T(8,128)} broadcast(f32[96,256]{1,0:T(8,128)} %param.12), dimensions={1,2} | broadcast | bytes 1671168 | tf_op jit(solution)/shard_map/broadcast_in_dim | solution.py:32
  2.3 7.6 %all-to-all-start = ((f32[16,96,256]{2,1,0:T(8,128)}), f32[16,96,256]{2,1,0:T(8,128)S(1)}, u32[]{:S(2)}, u32[]{:S(2)}) async-start(f32[16,96,256]{2,1,0:T(8,128)} %broadcast_in_dim.68), calls=%async_computation | async-start | bytes 3145728 | tf_op jit(solution)/shard_map/all_to_all | solution.py:27
  9.9 0.0 copy-done.13
  9.9 0.6 dynamic_slice.14
  10.5 0.6 fusion.36
  11.2 0.0 copy-done.9
  11.2 0.1 dynamic-slice_reduce_fusion.2
  11.3 0.1 slice.104
  11.4 0.1 broadcast_in_dim.63
  11.5 0.1 slice.106
  11.6 0.1 broadcast_in_dim.65
  11.7 0.1 slice.99
  11.8 0.1 broadcast_in_dim.58
  11.9 0.1 slice.96
  12.0 0.1 broadcast_in_dim.56
  12.1 0.1 slice.108
  12.2 0.1 broadcast_in_dim.67
  12.2 0.1 slice.102
  12.3 0.1 broadcast_in_dim.60
  12.4 0.0 copy-done.11
  12.4 0.1 broadcast_in_dim.61
  12.5 0.1 add.184
  12.6 0.0 copy-done.8
  12.6 0.1 slice_reduce_fusion.2
  12.7 6.6 %fusion.3 = (f32[1536,512]{1,0:T(8,128)}, f32[1536,512]{1,0:T(8,128)}) fusion(f32[512]{0:T(512)S(1)} %broadcast_in_dim.67, f32[512]{0:T(512)S(1)} %broadcast_in_dim.65, f32[512]{0:T(512)S(1)} %broadcast_in_dim.63, f32[1536]{0:T(1024)S(1)} %fusion.36, f32[512]{0:T(512)S(1)} %add.184, f32[1536]{0:T(1024)S(1)} %get-tuple-element.14, ...), kind=kLoop, calls=%fused_computation.11 | loop fusion | flops 34603008 | bytes 6330368 | tf_op jit(solution)/shard_map/mul | solution.py:80
  19.3 6.8 %fusion.7 = (f32[512,1536]{1,0:T(8,128)}, f32[512,1536]{1,0:T(8,128)}) fusion(f32[512]{0:T(512)S(1)} %broadcast_in_dim.67, f32[512]{0:T(512)S(1)} %broadcast_in_dim.65, f32[512]{0:T(512)S(1)} %broadcast_in_dim.63, f32[1536]{0:T(1024)S(1)} %fusion.36, f32[512]{0:T(512)S(1)} %add.184, f32[1536]{0:T(1024)S(1)} %get-tuple-element.14, ...), kind=kLoop, calls=%fused_computation.15 | loop fusion | flops 34603008 | bytes 6330368 | tf_op jit(solution)/shard_map/mul | solution.py:84
  26.1 3.7 %all-to-all-done = f32[16,96,256]{2,1,0:T(8,128)S(1)} async-done(((f32[16,96,256]{2,1,0:T(8,128)}), f32[16,96,256]{2,1,0:T(8,128)S(1)}, u32[]{:S(2)}, u32[]{:S(2)}) %all-to-all-start) | async-done | bytes 1572896 | tf_op jit(solution)/shard_map/all_to_all | solution.py:27
  29.8 3.5 %fusion.41 = f32[512,256]{1,0:T(8,128)S(1)} fusion(f32[512,1536]{1,0:T(8,128)} %get-tuple-element.11, f32[1536,256]{1,0:T(8,128)S(1)} %bitcast.39), kind=kOutput, calls=%fused_computation.79 | convolution fusion | flops 1207959552 | bytes 5242880 | tf_op jit(solution)/shard_map/dot_general | solution.py:94
  33.3 0.0 copy-start.4
  33.3 0.0 copy-start.5
  33.3 6.4 %collective-permute-start = (f32[512,256]{1,0:T(8,128)S(1)}, f32[512,256]{1,0:T(8,128)S(1)}, u32[]{:S(2)}, u32[]{:S(2)}) collective-permute-start(f32[512,256]{1,0:T(8,128)S(1)} %fusion.41), channel_id=1, source_target_pairs={{0,16},{16,0},{1,17},{17,1},{2,18},{18,2},{3,19},{19,3},{4,20},{20... | collective-permute-start | bytes 1572872 | tf_op jit(solution)/shard_map/ppermute | solution.py:36
  39.7 0.0 copy-done.2
  39.7 1.4 fusion.40
  41.1 0.0 copy-start.7
  41.1 0.0 collective-permute-done
  41.2 0.9 add.221
  42.1 6.1 %all-to-all-start.1 = ((f32[4,128,256]{2,1,0:T(8,128)}), f32[4,128,256]{2,1,0:T(8,128)S(1)}, u32[]{:S(2)}, u32[]{:S(2)}) async-start(f32[4,128,256]{2,1,0:T(8,128)} %bitcast.2), calls=%async_computation.1 | async-start | bytes 1048576 | tf_op jit(solution)/shard_map/all_to_all | solution.py:27
  48.2 0.9 dynamic-slice_multiply_fusion
  49.2 0.4 fusion.19
  49.5 0.4 fusion.21
  49.9 12.3 %all-to-all-done.1 = f32[4,128,256]{2,1,0:T(8,128)S(1)} async-done(((f32[4,128,256]{2,1,0:T(8,128)}), f32[4,128,256]{2,1,0:T(8,128)S(1)}, u32[]{:S(2)}, u32[]{:S(2)}) %all-to-all-start.1) | async-done | bytes 524320 | tf_op jit(solution)/shard_map/all_to_all | solution.py:27
  62.3 31.0 %all-gather = f32[512,256]{1,0:T(8,128)S(1)} all-gather(f32[128,256]{1,0:T(8,128)S(1)} %reduce_sum.36), channel_id=2, replica_groups=mesh['far'=4,'near'=4,'core'=2,'kvec'=16] {'far'}, dimensions={0}, use_global_device_ids=true | all-gather | bytes 655360 | tf_op jit(solution)/shard_map/all_gather | solution.py:97
  93.3 0.0 copy-start.1
  93.3 0.0 copy-done.7
  93.3 0.3 fusion.17
  93.7 0.3 fusion.42
  94.0 0.3 convolution_add_fusion.1
  94.3 16.7 %all_to_all.20 = f32[4,128,256]{2,1,0:T(8,128)S(1)} all-to-all(f32[4,128,256]{2,1,0:T(8,128)S(1)} %broadcast_in_dim.69), channel_id=1, replica_groups=mesh['far'=4,'near'=4,'core'=2,'kvec'=16] {'near'}, dimensions={0} | all-to-all | bytes 1048576 | tf_op jit(solution)/shard_map/all_to_all | solution.py:27
  111.0 3.8 %collective-permute-start.1 = (f32[512,256]{1,0:T(8,128)S(1)}, f32[512,256]{1,0:T(8,128)S(1)}, u32[]{:S(2)}, u32[]{:S(2)}) collective-permute-start(f32[512,256]{1,0:T(8,128)S(1)} %bitcast.42), channel_id=1, source_target_pairs={{0,16},{16,0},{1,17},{17,1},{2,18},{18,2},{3,19},{19,3},{4,20},{20... | collective-permute-start | bytes 1572872 | tf_op jit(solution)/shard_map/ppermute | solution.py:36
  114.9 0.0 copy-done.1
  114.9 1.5 fusion.43
  116.3 0.0 collective-permute-done.1
  116.4 0.0 copy-done.3
  116.4 2.6 %convolution_add_fusion = f32[1536,256]{1,0:T(8,128)} fusion(f32[1536,256]{1,0:T(8,128)S(1)} %fusion.43, f32[1536,512]{1,0:T(8,128)S(1)} %copy-done.3, f32[512,256]{1,0:T(8,128)S(1)} %collective-permute-done.1), kind=kOutput, calls=%fused_computation.32 | convolution fusion | flops 1208352768 | bytes 6815744 | tf_op jit(solution)/shard_map/dot_general | solution.py:111
  119.0 4.2 %all-to-all-start.3 = ((f32[16,96,256]{2,1,0:T(8,128)}), f32[16,96,256]{2,1,0:T(8,128)S(1)}, u32[]{:S(2)}, u32[]{:S(2)}) async-start(f32[16,96,256]{2,1,0:T(8,128)} %bitcast.41), calls=%async_computation.3 | async-start | bytes 3145728 | tf_op jit(solution)/shard_map/all_to_all | solution.py:27
  123.2 0.7 compare_convert_fusion
  123.8 21.5 %all-to-all-done.3 = f32[16,96,256]{2,1,0:T(8,128)S(1)} async-done(((f32[16,96,256]{2,1,0:T(8,128)}), f32[16,96,256]{2,1,0:T(8,128)S(1)}, u32[]{:S(2)}, u32[]{:S(2)}) %all-to-all-start.3) | async-done | bytes 1572896 | tf_op jit(solution)/shard_map/all_to_all | solution.py:27
  145.3 0.1 reduce_sum.38
  145.4 0.1 multiply_reduce_fusion
  145.5 0.5 fusion.31
  146.0 1.1 fusion.16
  (28 shorter events, 0.3 us)
Async XLA Ops:
  0.0 145.5 %copy-start = (f32[256,512]{1,0:T(8,128)S(1)}, f32[256,512]{1,0:T(8,128)}, u32[]{:S(2)}) copy-start(f32[256,512]{1,0:T(8,128)} %param.21) | copy-start | bytes 1572868
  0.0 12.4 %copy-start.11 = (f32[2]{0:T(128)S(1)}, f32[2]{0:T(128)}, u32[]{:S(2)}) copy-start(f32[2]{0:T(128)} %constant.73.clone) | copy-start | bytes 28
  0.0 9.9 %copy-start.13 = (s32[32]{0:T(128)S(1)}, s32[32]{0:T(128)}, u32[]{:S(2)}) copy-start(s32[32]{0:T(128)} %param.15) | copy-start | bytes 388
  0.0 11.2 %copy-start.9 = (s32[3,512]{1,0:T(4,128)S(1)}, s32[3,512]{1,0:T(4,128)}, u32[]{:S(2)}) copy-start(s32[3,512]{1,0:T(4,128)} %param.14) | copy-start | bytes 18436
  0.0 12.6 %copy-start.8 = (s32[3,1536]{1,0:T(4,128)S(1)}, s32[3,1536]{1,0:T(4,128)}, u32[]{:S(2)}) copy-start(s32[3,1536]{1,0:T(4,128)} %param.13) | copy-start | bytes 55300
  2.3 27.5 %all-to-all-start = ((f32[16,96,256]{2,1,0:T(8,128)}), f32[16,96,256]{2,1,0:T(8,128)S(1)}, u32[]{:S(2)}, u32[]{:S(2)}) async-start(f32[16,96,256]{2,1,0:T(8,128)} %broadcast_in_dim.68), calls=%async_computation | async-start | bytes 3145728 | tf_op jit(solution)/shard_map/all_to_all | solution.py:27
  29.8 9.9 %copy-start.2 = (f32[512,1536]{1,0:T(8,128)S(1)}, f32[512,1536]{1,0:T(8,128)}, u32[]{:S(2)}) copy-start(f32[512,1536]{1,0:T(8,128)} %get-tuple-element.10) | copy-start | bytes 9437188
  33.3 15.9 %copy-start.4 = (f32[256,256]{1,0:T(8,128)S(1)}, f32[256,256]{1,0:T(8,128)}, u32[]{:S(2)}) copy-start(f32[256,256]{1,0:T(8,128)} %param.19) | copy-start | bytes 786436
  33.3 15.9 %copy-start.5 = (f32[2,256,256]{2,1,0:T(8,128)S(1)}, f32[2,256,256]{2,1,0:T(8,128)}, u32[]{:S(2)}) copy-start(f32[2,256,256]{2,1,0:T(8,128)} %param.18) | copy-start | bytes 1572868
  33.3 7.9 %collective-permute-start = (f32[512,256]{1,0:T(8,128)S(1)}, f32[512,256]{1,0:T(8,128)S(1)}, u32[]{:S(2)}, u32[]{:S(2)}) collective-permute-start(f32[512,256]{1,0:T(8,128)S(1)} %fusion.41), channel_id=1, source_target_pairs={{0,16},{16,0},{1,17},{17,1},{2,18},{18,2},{3,19},{19,3},{4,20},{20... | collective-permute-start | bytes 1572872 | tf_op jit(solution)/shard_map/ppermute | solution.py:36
  41.1 52.2 %copy-start.7 = (f32[256,256]{1,0:T(8,128)S(1)}, f32[256,256]{1,0:T(8,128)}, u32[]{:S(2)}) copy-start(f32[256,256]{1,0:T(8,128)} %param.16) | copy-start | bytes 786436
  42.1 20.2 %all-to-all-start.1 = ((f32[4,128,256]{2,1,0:T(8,128)}), f32[4,128,256]{2,1,0:T(8,128)S(1)}, u32[]{:S(2)}, u32[]{:S(2)}) async-start(f32[4,128,256]{2,1,0:T(8,128)} %bitcast.2), calls=%async_computation.1 | async-start | bytes 1048576 | tf_op jit(solution)/shard_map/all_to_all | solution.py:27
  93.3 21.5 %copy-start.1 = (f32[1536,512]{1,0:T(8,128)S(1)}, f32[1536,512]{1,0:T(8,128)}, u32[]{:S(2)}) copy-start(f32[1536,512]{1,0:T(8,128)} %get-tuple-element.9) | copy-start | bytes 9437188
  94.3 22.1 %copy-start.3 = (f32[1536,512]{1,0:T(8,128)S(1)}, f32[1536,512]{1,0:T(8,128)}, u32[]{:S(2)}) copy-start(f32[1536,512]{1,0:T(8,128)} %get-tuple-element.12) | copy-start | bytes 9437188
  111.0 5.4 %collective-permute-start.1 = (f32[512,256]{1,0:T(8,128)S(1)}, f32[512,256]{1,0:T(8,128)S(1)}, u32[]{:S(2)}, u32[]{:S(2)}) collective-permute-start(f32[512,256]{1,0:T(8,128)S(1)} %bitcast.42), channel_id=1, source_target_pairs={{0,16},{16,0},{1,17},{17,1},{2,18},{18,2},{3,19},{19,3},{4,20},{20... | collective-permute-start | bytes 1572872 | tf_op jit(solution)/shard_map/ppermute | solution.py:36
  119.0 26.4 %copy-start.6 = (f32[96,256]{1,0:T(8,128)S(1)}, f32[96,256]{1,0:T(8,128)}, u32[]{:S(2)}) copy-start(f32[96,256]{1,0:T(8,128)} %param.12) | copy-start | bytes 294916
  119.0 26.6 %copy-start.10 = (f32[256]{0:T(256)S(1)}, f32[256]{0:T(256)}, u32[]{:S(2)}) copy-start(f32[256]{0:T(256)} %param.20) | copy-start | bytes 3076
  119.0 27.0 %copy-start.12 = (f32[512,256]{1,0:T(8,128)S(1)}, f32[512,256]{1,0:T(8,128)}, u32[]{:S(2)}) copy-start(f32[512,256]{1,0:T(8,128)} %param.22) | copy-start | bytes 1572868
  119.0 26.3 %all-to-all-start.3 = ((f32[16,96,256]{2,1,0:T(8,128)}), f32[16,96,256]{2,1,0:T(8,128)S(1)}, u32[]{:S(2)}, u32[]{:S(2)}) async-start(f32[16,96,256]{2,1,0:T(8,128)} %bitcast.41), calls=%async_computation.3 | async-start | bytes 3145728 | tf_op jit(solution)/shard_map/all_to_all | solution.py:27

commit v3 on v2

--- a/solution.py
+++ b/solution.py
@@ -9,6 +9,9 @@
 exact = lax.Precision.HIGHEST
 high = lax.Precision.HIGH
 NEAR = 4
+SIDE = 4
+PLANE = [[i * SIDE + (i + d) % SIDE for d in range(SIDE) for i in range(SIDE)]]
+LOOP = [[0, 1, 3, 2]]
 
 SIN_HALF = (3.1415926401307073, -5.167710083507923, 2.5500775232148563, -0.5982912856211671, 0.07765766030589402)
 
@@ -23,13 +26,13 @@
     return 1.0 - (s + s) * s
 
 
-def exchange(blocks, axes):
-    return lax.all_to_all(blocks, axes, 0, 0, tiled=True)
+def exchange(blocks, axes, sets=None):
+    return lax.all_to_all(blocks, axes, 0, 0, axis_index_groups=sets, tiled=True)
 
 
-def to_all(block, axes):
+def to_all(block, axes, sets=None):
     peers = lax.axis_size(axes)
-    return exchange(jnp.broadcast_to(block[None], (peers, *block.shape)), axes)
+    return exchange(jnp.broadcast_to(block[None], (peers, *block.shape)), axes, sets)
 
 
 def swap_cores(block):
@@ -64,10 +67,13 @@
     own_brick = (lax.axis_index("far") * near + lax.axis_index("near")) * 2 + core
     count = lax.dynamic_index_in_dim(brick_count, own_brick, 0, False)
 
-    values = to_all(features, "kvec").reshape(capacity, width)
+    values = to_all(features, "kvec", PLANE).reshape(capacity, width)
 
-    live = (jnp.arange(capacity, dtype=jnp.int32) < count).astype(jnp.float32)
-    fracs = fractions.astype(jnp.float32)
+    def in_order(slots):
+        return jnp.concatenate([slots[..., g * share : (g + 1) * share] for g in PLANE[0]], axis=-1)
+
+    live = in_order((jnp.arange(capacity, dtype=jnp.int32) < count).astype(jnp.float32))
+    fracs = in_order(fractions.astype(jnp.float32))
     waves = wave_index.astype(jnp.float32) * (1.0 / 1024.0)
     quarter = jnp.broadcast_to(jnp.array([0.0, 0.25], jnp.float32)[None, :, None], (rings, 2, k_own)).reshape(-1)
 
@@ -83,9 +89,12 @@
         turns = sum(w[j][:, None] * fracs[j][None, :] for j in range(3)) + quarter[:, None]
         return cos_turns(turns) * live[None, :]
 
+    def looped(w):
+        return jnp.concatenate([jnp.split(w, near, axis=1)[n] for n in LOOP[0]], axis=1)
+
     w_own, w_other = lines(core), lines(1 - core)
     own, other, own_t, other_t = lax.optimization_barrier(
-        (basis(w_own), basis(w_other), basis_t(w_own), basis_t(w_other))
+        (basis(w_own), basis(w_other), basis_t(looped(w_own)), basis_t(looped(w_other)))
     )
     out_mix = jnp.stack(
         [jnp.dot(mix_weight[0], out_weight, precision=exact), jnp.dot(mix_weight[1], out_weight, precision=exact)]
@@ -93,7 +102,7 @@
 
     passed = swap_cores(jnp.dot(other_t, values, precision=high))
     summed = lax.optimization_barrier(jnp.dot(own_t, values, precision=high)) + passed
-    close = jnp.sum(exchange(summed.reshape(near, far * rows, width), "near"), axis=0)
+    close = jnp.sum(exchange(summed.reshape(near, far * rows, width), "near", LOOP), axis=0)
     raw = jnp.sum(lax.all_gather(close, "far", axis=0), axis=0)
     total = jnp.dot(raw, value_weight, precision=exact).reshape(far, 2, k_own, width)
     real_sf, imag_sf = total[:, 0], total[:, 1]
@@ -106,10 +115,10 @@
         jnp.stack([-u_im, u_re], axis=1).reshape(far * rows, width), out_mix[1], precision=exact
     )
 
-    t_own = to_all(mixed, "near").reshape(rings * rows, width)
+    t_own = lax.all_gather(mixed, "near", axis=0, tiled=True)
     t_other = swap_cores(t_own)
     messages = jnp.dot(own, t_own, precision=high) + jnp.dot(other, t_other, precision=high)
-    landed = exchange(messages.reshape(groups, share, width), "kvec")
+    landed = exchange(messages.reshape(groups, share, width), "kvec", PLANE)
     residual = features + jnp.sum(landed, axis=0)
     normed = residual * lax.rsqrt(jnp.mean(residual * residual, axis=1, keepdims=True) + 1e-06) * norm_gain
     hidden = jax.nn.silu(jnp.dot(normed, up_weight, precision=exact))

time: 148 us -> 145 us (0.980)
  waiting for transfers between devices: 37.6 us -> 35.1 us
  starting transfers between devices: 28.1 us -> 26.4 us
    all_gather x0 -> x1, blocking collectives: none -> 18.3 us  [shards(): t_own = lax.all_gather(mixed, 'near', axis=0, tiled=True)]
    all_to_all x1 -> x0, blocking collectives: 16.7 us -> none  [exchange(): return lax.all_to_all(blocks, axes, 0, 0, tiled=True)]
    all_to_all x3, waiting for transfers between devices: 37.5 us -> 35 us  [exchange(): lax.all_to_all(blocks, axes, 0, 0, axis_index_groups=sets, tiled=True)]
    all_gather x1, blocking collectives: 31 us -> 28.8 us  [shards(): raw = jnp.sum(lax.all_gather(close, 'far', axis=0), axis=0)]
    ppermute x2, starting transfers between devices: 10.2 us -> 8.12 us  [swap_cores(): return lax.ppermute(block, 'core', [(0, 1), (1, 0)])]
  transfers between devices with their start and end apart: 5 -> 5, of which waited for: 3 -> 3; matrix products, arithmetic and copies ran while one was open for 14% -> 16% of each run, Pallas kernels for 0% -> 0%
where the time goes in v3:
time: 145 us; the launch traced here: 143 us
  blocking collectives  47.1 us (32%)
  waiting for transfers between devices  35.1 us (24%)
  starting transfers between devices  26.4 us (18%)
  other arithmetic  16.9 us (12%)
  matrix products  12 us (8%)
  local copies, waits for them, and re-layouts  5.31 us (4%)
    all_to_all x3, waiting for transfers between devices, exchange(): lax.all_to_all(blocks, axes, 0, 0, axis_index_groups=sets, tiled=True)  35 us
    all_gather x1, blocking collectives, shards(): raw = jnp.sum(lax.all_gather(close, 'far', axis=0), axis=0)  28.8 us
    all_to_all x3, starting transfers between devices, exchange(): lax.all_to_all(blocks, axes, 0, 0, axis_index_groups=sets, tiled=True)  18.3 us
    all_gather x1, blocking collectives, shards(): t_own = lax.all_gather(mixed, 'near', axis=0, tiled=True)  18.3 us
    ppermute x2, starting transfers between devices, swap_cores(): return lax.ppermute(block, 'core', [(0, 1), (1, 0)])  8.12 us
    mul x1, other arithmetic, basis_t(): return cos_turns(turns) * live[None, :]  6.84 us
    mul x1, other arithmetic, basis(): return cos_turns(turns) * live[:, None]  6.63 us
    dot_general x1, matrix products, shards(): passed = swap_cores(jnp.dot(other_t, values, precision=high))  3.46 us
  transfers between devices with their start and end apart: 5, of which 3 were waited for; matrix products, arithmetic and copies ran while one was open for 16% of the time, Pallas kernels for 0%

profile of v3, /device:TPU:1, one launch (start us, length us, event | category | flops | bytes accessed | tf_op | source)
XLA Modules:
  0.0 143.3 jit_solution(17058847562299608743)
XLA Ops:
  0.0 2.3 %broadcast_in_dim.74 = f32[16,96,256]{2,1,0:T(8,128)} broadcast(f32[96,256]{1,0:T(8,128)} %param.12), dimensions={1,2} | broadcast | bytes 1671168 | tf_op jit(solution)/shard_map/broadcast_in_dim | solution.py:35
  2.3 7.6 %all-to-all-start = ((f32[16,96,256]{2,1,0:T(8,128)}), f32[16,96,256]{2,1,0:T(8,128)S(1)}, u32[]{:S(2)}, u32[]{:S(2)}) async-start(f32[16,96,256]{2,1,0:T(8,128)} %broadcast_in_dim.74), calls=%async_computation | async-start | bytes 3145728 | tf_op jit(solution)/shard_map/all_to_all | solution.py:30
  9.9 0.6 dynamic_slice.14
  10.5 0.6 fusion.36
  11.2 0.1 fusion.47
  11.3 0.1 fusion.46
  11.4 0.1 fusion.43
  11.4 0.1 fusion.42
  11.5 0.1 fusion.38
  11.6 0.1 slice.234
  11.7 0.1 broadcast_in_dim.65
  11.8 0.1 slice.238
  11.9 0.1 broadcast_in_dim.69
  12.0 0.1 slice.236
  12.1 0.1 broadcast_in_dim.67
  12.2 0.1 slice.219
  12.3 0.1 broadcast_in_dim.62
  12.4 0.1 slice.216
  12.5 0.1 broadcast_in_dim.60
  12.6 0.1 slice.213
  12.7 0.1 broadcast_in_dim.58
  12.8 0.1 broadcast_in_dim.63
  12.8 0.1 add.184
  12.9 0.1 broadcast_in_dim.72
  13.0 0.1 concatenate.16
  13.1 0.1 slice_reduce_fusion.2
  13.2 0.1 reshape.105
  13.3 0.1 broadcast_in_dim.70
  13.5 0.1 reshape.104
  13.6 0.1 concatenate.17
  13.7 6.6 %fusion.3 = (f32[1536,512]{1,0:T(8,128)}, f32[1536,512]{1,0:T(8,128)}) fusion(f32[512]{0:T(512)S(1)} %broadcast_in_dim.69, f32[512]{0:T(512)S(1)} %broadcast_in_dim.67, f32[512]{0:T(512)S(1)} %broadcast_in_dim.65, f32[1536]{0:T(1024)S(1)} %concatenate.17, f32[512]{0:T(512)S(1)} %add.184, f32[1536]{0:T(1024)S(1)} %get-tuple-element.14, ...), kind=kLoop, calls=%fused_computation.11 | loop fusion | flops 34603008 | bytes 6330368 | tf_op jit(solution)/shard_map/mul | solution.py:86
  20.3 6.8 %fusion.7 = (f32[512,1536]{1,0:T(8,128)}, f32[512,1536]{1,0:T(8,128)}) fusion(f32[512]{0:T(512)S(1)} %bitcast.55, f32[512]{0:T(512)S(1)} %bitcast.54, f32[512]{0:T(512)S(1)} %bitcast.53, f32[1536]{0:T(1024)S(1)} %concatenate.17, f32[512]{0:T(512)S(1)} %add.184, f32[1536]{0:T(1024)S(1)} %get-tuple-element.14, f32[1536]{0:T(1024)S(1)} %get-tuple-element.15, ...), kind=kLoop, calls=%fused_computation.15 | loop fusion | flops 34603008 | bytes 6330368 | tf_op jit(solution)/shard_map/mul | solution.py:90
  27.2 4.2 %all-to-all-done = f32[16,96,256]{2,1,0:T(8,128)S(1)} async-done(((f32[16,96,256]{2,1,0:T(8,128)}), f32[16,96,256]{2,1,0:T(8,128)S(1)}, u32[]{:S(2)}, u32[]{:S(2)}) %all-to-all-start) | async-done | bytes 1572896 | tf_op jit(solution)/shard_map/all_to_all | solution.py:30
  31.4 3.5 %fusion.49 = f32[512,256]{1,0:T(8,128)S(1)} fusion(f32[512,1536]{1,0:T(8,128)} %get-tuple-element.11, f32[1536,256]{1,0:T(8,128)S(1)} %bitcast.44), kind=kOutput, calls=%fused_computation.97 | convolution fusion | flops 1207959552 | bytes 5242880 | tf_op jit(solution)/shard_map/dot_general | solution.py:103
  34.9 0.0 copy-start.4
  34.9 0.0 copy-start.5
  34.9 4.0 %collective-permute-start = (f32[512,256]{1,0:T(8,128)S(1)}, f32[512,256]{1,0:T(8,128)S(1)}, u32[]{:S(2)}, u32[]{:S(2)}) collective-permute-start(f32[512,256]{1,0:T(8,128)S(1)} %fusion.49), channel_id=1, source_target_pairs={{0,16},{16,0},{1,17},{17,1},{2,18},{18,2},{3,19},{19,3},{4,20},{20... | collective-permute-start | bytes 1572872 | tf_op jit(solution)/shard_map/ppermute | solution.py:39
  38.9 0.0 copy-done.2
  38.9 1.4 %fusion.48 = f32[512,256]{1,0:T(8,128)S(1)} fusion(f32[512,1536]{1,0:T(8,128)S(1)} %copy-done.2, f32[1536,256]{1,0:T(8,128)S(1)} %bitcast.45), kind=kOutput, calls=%fused_computation.96 | convolution fusion | flops 1207959552 | bytes 5242880 | tf_op jit(solution)/shard_map/dot_general | solution.py:104
  40.3 0.0 copy-start.7
  40.3 0.0 collective-permute-done
  40.4 0.9 add.221
  41.3 4.7 %all-to-all-start.1 = ((f32[4,128,256]{2,1,0:T(8,128)}), f32[4,128,256]{2,1,0:T(8,128)S(1)}, u32[]{:S(2)}, u32[]{:S(2)}) async-start(f32[4,128,256]{2,1,0:T(8,128)} %bitcast.8), calls=%async_computation.1 | async-start | bytes 1048576 | tf_op jit(solution)/shard_map/all_to_all | solution.py:30
  46.0 0.9 dynamic-slice_multiply_fusion
  46.9 0.4 fusion.19
  47.3 0.4 fusion.21
  47.7 10.3 %all-to-all-done.1 = f32[4,128,256]{2,1,0:T(8,128)S(1)} async-done(((f32[4,128,256]{2,1,0:T(8,128)}), f32[4,128,256]{2,1,0:T(8,128)S(1)}, u32[]{:S(2)}, u32[]{:S(2)}) %all-to-all-start.1) | async-done | bytes 524320 | tf_op jit(solution)/shard_map/all_to_all | solution.py:30
  58.1 28.8 %all-gather = f32[512,256]{1,0:T(8,128)S(1)} all-gather(f32[128,256]{1,0:T(8,128)S(1)} %reduce_sum.36), channel_id=2, replica_groups=mesh['far'=4,'near'=4,'core'=2,'kvec'=16] {'far'}, dimensions={0}, use_global_device_ids=true | all-gather | bytes 655360 | tf_op jit(solution)/shard_map/all_gather | solution.py:106
  86.9 0.3 fusion.17
  87.3 0.3 fusion.50
  87.6 0.3 convolution_add_fusion.1
  87.9 18.3 %all_gather.11 = f32[512,256]{1,0:T(8,128)S(1)} all-gather(f32[128,256]{1,0:T(8,128)S(1)} %convolution_add_fusion.1), channel_id=1, replica_groups=mesh['far'=4,'near'=4,'core'=2,'kvec'=16] {'near'}, dimensions={0}, use_global_device_ids=true | all-gather | bytes 655360 | tf_op jit(solution)/shard_map/all_gather | solution.py:118
  106.1 4.1 %collective-permute-start.1 = (f32[512,256]{1,0:T(8,128)S(1)}, f32[512,256]{1,0:T(8,128)S(1)}, u32[]{:S(2)}, u32[]{:S(2)}) collective-permute-start(f32[512,256]{1,0:T(8,128)S(1)} %all_gather.11), channel_id=1, source_target_pairs={{0,16},{16,0},{1,17},{17,1},{2,18},{18,2},{3,19},{19,3},{4,20},{20... | collective-permute-start | bytes 1572872 | tf_op jit(solution)/shard_map/ppermute | solution.py:39
  110.3 0.0 copy-done.1
  110.3 1.4 fusion.51
  111.7 0.0 collective-permute-done.1
  111.7 2.6 %convolution_add_fusion = f32[1536,256]{1,0:T(8,128)} fusion(f32[1536,256]{1,0:T(8,128)S(1)} %fusion.51, f32[1536,512]{1,0:T(8,128)S(1)} %copy-done.3, f32[512,256]{1,0:T(8,128)S(1)} %collective-permute-done.1), kind=kOutput, calls=%fused_computation.32 | convolution fusion | flops 1208352768 | bytes 6815744 | tf_op jit(solution)/shard_map/dot_general | solution.py:120
  114.3 6.0 %all-to-all-start.2 = ((f32[16,96,256]{2,1,0:T(8,128)}), f32[16,96,256]{2,1,0:T(8,128)S(1)}, u32[]{:S(2)}, u32[]{:S(2)}) async-start(f32[16,96,256]{2,1,0:T(8,128)} %bitcast.46), calls=%async_computation.2 | async-start | bytes 3145728 | tf_op jit(solution)/shard_map/all_to_all | solution.py:30
  120.3 0.7 compare_convert_fusion
  121.0 20.5 %all-to-all-done.2 = f32[16,96,256]{2,1,0:T(8,128)S(1)} async-done(((f32[16,96,256]{2,1,0:T(8,128)}), f32[16,96,256]{2,1,0:T(8,128)S(1)}, u32[]{:S(2)}, u32[]{:S(2)}) %all-to-all-start.2) | async-done | bytes 1572896 | tf_op jit(solution)/shard_map/all_to_all | solution.py:30
  141.5 0.1 reduce_sum.38
  141.6 0.1 multiply_reduce_fusion
  141.7 0.5 fusion.31
  142.2 1.1 fusion.16
  (46 shorter events, 0.3 us)
Async XLA Ops:
  0.0 141.7 %copy-start = (f32[256,512]{1,0:T(8,128)S(1)}, f32[256,512]{1,0:T(8,128)}, u32[]{:S(2)}) copy-start(f32[256,512]{1,0:T(8,128)} %param.21) | copy-start | bytes 1572868
  0.0 12.8 %copy-start.11 = (f32[2]{0:T(128)S(1)}, f32[2]{0:T(128)}, u32[]{:S(2)}) copy-start(f32[2]{0:T(128)} %constant.73.clone) | copy-start | bytes 28
  0.0 9.9 %copy-start.13 = (s32[32]{0:T(128)S(1)}, s32[32]{0:T(128)}, u32[]{:S(2)}) copy-start(s32[32]{0:T(128)} %param.15) | copy-start | bytes 388
  0.0 11.3 %copy-start.8 = (s32[3,1536]{1,0:T(4,128)S(1)}, s32[3,1536]{1,0:T(4,128)}, u32[]{:S(2)}) copy-start(s32[3,1536]{1,0:T(4,128)} %param.13) | copy-start | bytes 55300
  0.0 11.5 %copy-start.9 = (s32[3,512]{1,0:T(4,128)S(1)}, s32[3,512]{1,0:T(4,128)}, u32[]{:S(2)}) copy-start(s32[3,512]{1,0:T(4,128)} %param.14) | copy-start | bytes 18436
  2.3 29.1 %all-to-all-start = ((f32[16,96,256]{2,1,0:T(8,128)}), f32[16,96,256]{2,1,0:T(8,128)S(1)}, u32[]{:S(2)}, u32[]{:S(2)}) async-start(f32[16,96,256]{2,1,0:T(8,128)} %broadcast_in_dim.74), calls=%async_computation | async-start | bytes 3145728 | tf_op jit(solution)/shard_map/all_to_all | solution.py:30
  31.4 7.5 %copy-start.2 = (f32[512,1536]{1,0:T(8,128)S(1)}, f32[512,1536]{1,0:T(8,128)}, u32[]{:S(2)}) copy-start(f32[512,1536]{1,0:T(8,128)} %get-tuple-element.10) | copy-start | bytes 9437188
  34.9 12.1 %copy-start.4 = (f32[256,256]{1,0:T(8,128)S(1)}, f32[256,256]{1,0:T(8,128)}, u32[]{:S(2)}) copy-start(f32[256,256]{1,0:T(8,128)} %param.19) | copy-start | bytes 786436
  34.9 12.0 %copy-start.5 = (f32[2,256,256]{2,1,0:T(8,128)S(1)}, f32[2,256,256]{2,1,0:T(8,128)}, u32[]{:S(2)}) copy-start(f32[2,256,256]{2,1,0:T(8,128)} %param.18) | copy-start | bytes 1572868
  34.9 5.5 %collective-permute-start = (f32[512,256]{1,0:T(8,128)S(1)}, f32[512,256]{1,0:T(8,128)S(1)}, u32[]{:S(2)}, u32[]{:S(2)}) collective-permute-start(f32[512,256]{1,0:T(8,128)S(1)} %fusion.49), channel_id=1, source_target_pairs={{0,16},{16,0},{1,17},{17,1},{2,18},{18,2},{3,19},{19,3},{4,20},{20... | collective-permute-start | bytes 1572872 | tf_op jit(solution)/shard_map/ppermute | solution.py:39
  40.3 46.6 %copy-start.7 = (f32[256,256]{1,0:T(8,128)S(1)}, f32[256,256]{1,0:T(8,128)}, u32[]{:S(2)}) copy-start(f32[256,256]{1,0:T(8,128)} %param.16) | copy-start | bytes 786436
  41.3 16.8 %all-to-all-start.1 = ((f32[4,128,256]{2,1,0:T(8,128)}), f32[4,128,256]{2,1,0:T(8,128)S(1)}, u32[]{:S(2)}, u32[]{:S(2)}) async-start(f32[4,128,256]{2,1,0:T(8,128)} %bitcast.8), calls=%async_computation.1 | async-start | bytes 1048576 | tf_op jit(solution)/shard_map/all_to_all | solution.py:30
  86.9 23.4 %copy-start.1 = (f32[1536,512]{1,0:T(8,128)S(1)}, f32[1536,512]{1,0:T(8,128)}, u32[]{:S(2)}) copy-start(f32[1536,512]{1,0:T(8,128)} %get-tuple-element.9) | copy-start | bytes 9437188
  87.6 24.1 %copy-start.3 = (f32[1536,512]{1,0:T(8,128)S(1)}, f32[1536,512]{1,0:T(8,128)}, u32[]{:S(2)}) copy-start(f32[1536,512]{1,0:T(8,128)} %get-tuple-element.12) | copy-start | bytes 9437188
  106.1 5.6 %collective-permute-start.1 = (f32[512,256]{1,0:T(8,128)S(1)}, f32[512,256]{1,0:T(8,128)S(1)}, u32[]{:S(2)}, u32[]{:S(2)}) collective-permute-start(f32[512,256]{1,0:T(8,128)S(1)} %all_gather.11), channel_id=1, source_target_pairs={{0,16},{16,0},{1,17},{17,1},{2,18},{18,2},{3,19},{19,3},{4,20},{20... | collective-permute-start | bytes 1572872 | tf_op jit(solution)/shard_map/ppermute | solution.py:39
  114.3 27.3 %copy-start.6 = (f32[96,256]{1,0:T(8,128)S(1)}, f32[96,256]{1,0:T(8,128)}, u32[]{:S(2)}) copy-start(f32[96,256]{1,0:T(8,128)} %param.12) | copy-start | bytes 294916
  114.3 27.4 %copy-start.10 = (f32[256]{0:T(256)S(1)}, f32[256]{0:T(256)}, u32[]{:S(2)}) copy-start(f32[256]{0:T(256)} %param.20) | copy-start | bytes 3076
  114.3 27.9 %copy-start.12 = (f32[512,256]{1,0:T(8,128)S(1)}, f32[512,256]{1,0:T(8,128)}, u32[]{:S(2)}) copy-start(f32[512,256]{1,0:T(8,128)} %param.22) | copy-start | bytes 1572868
  114.3 27.2 %all-to-all-start.2 = ((f32[16,96,256]{2,1,0:T(8,128)}), f32[16,96,256]{2,1,0:T(8,128)S(1)}, u32[]{:S(2)}, u32[]{:S(2)}) async-start(f32[16,96,256]{2,1,0:T(8,128)} %bitcast.46), calls=%async_computation.2 | async-start | bytes 3145728 | tf_op jit(solution)/shard_map/all_to_all | solution.py:30

commit v4 on v3

--- a/solution.py
+++ b/solution.py
@@ -85,34 +85,42 @@
         turns = sum(fracs[j][:, None] * w[j][None, :] for j in range(3)) + quarter[None, :]
         return cos_turns(turns) * live[:, None]
 
-    def basis_t(w):
-        turns = sum(w[j][:, None] * fracs[j][None, :] for j in range(3)) + quarter[:, None]
-        return cos_turns(turns) * live[None, :]
+    def basis_t(w, slots):
+        turns = sum(w[j][:, None] * fracs[j][None, slots] for j in range(3)) + quarter[:, None]
+        return cos_turns(turns) * live[None, slots]
 
     def looped(w):
         return jnp.concatenate([jnp.split(w, near, axis=1)[n] for n in LOOP[0]], axis=1)
 
     w_own, w_other = lines(core), lines(1 - core)
+    parts = [slice(0, capacity // 2), slice(capacity // 2, capacity)]
     own, other, own_t, other_t = lax.optimization_barrier(
-        (basis(w_own), basis(w_other), basis_t(looped(w_own)), basis_t(looped(w_other)))
+        (
+            basis(w_own),
+            basis(w_other),
+            basis_t(looped(w_own), slice(0, capacity)),
+            [basis_t(looped(w_other), part) for part in parts],
+        )
     )
     out_mix = jnp.stack(
         [jnp.dot(mix_weight[0], out_weight, precision=exact), jnp.dot(mix_weight[1], out_weight, precision=exact)]
     )
 
-    passed = swap_cores(jnp.dot(other_t, values, precision=high))
+    passed = swap_cores(
+        sum(jnp.dot(basis_part, values[part], precision=high) for basis_part, part in zip(other_t, parts))
+    )
     summed = lax.optimization_barrier(jnp.dot(own_t, values, precision=high)) + passed
     close = jnp.sum(exchange(summed.reshape(near, far * rows, width), "near", LOOP), axis=0)
     raw = jnp.sum(lax.all_gather(close, "far", axis=0), axis=0)
-    total = jnp.dot(raw, value_weight, precision=exact).reshape(far, 2, k_own, width)
+    total = jnp.dot(raw, value_weight, precision=high).reshape(far, 2, k_own, width)
     real_sf, imag_sf = total[:, 0], total[:, 1]
     kept = far * k_own
     filt = lax.dynamic_slice_in_dim(k_filter, core * k_half + lax.axis_index("near") * kept, kept, 1) * normalizer
     filt = filt.reshape(2, far, k_own, width)
     u_re = real_sf * filt[0] - imag_sf * filt[1]
     u_im = real_sf * filt[1] + imag_sf * filt[0]
-    mixed = jnp.dot(jnp.stack([u_re, u_im], axis=1).reshape(far * rows, width), out_mix[0], precision=exact) + jnp.dot(
-        jnp.stack([-u_im, u_re], axis=1).reshape(far * rows, width), out_mix[1], precision=exact
+    mixed = jnp.dot(jnp.stack([u_re, u_im], axis=1).reshape(far * rows, width), out_mix[0], precision=high) + jnp.dot(
+        jnp.stack([-u_im, u_re], axis=1).reshape(far * rows, width), out_mix[1], precision=high
     )
 
     t_own = lax.all_gather(mixed, "near", axis=0, tiled=True)
@@ -121,10 +129,10 @@
     landed = exchange(messages.reshape(groups, share, width), "kvec", PLANE)
     residual = features + jnp.sum(landed, axis=0)
     normed = residual * lax.rsqrt(jnp.mean(residual * residual, axis=1, keepdims=True) + 1e-06) * norm_gain
-    hidden = jax.nn.silu(jnp.dot(normed, up_weight, precision=exact))
+    hidden = jax.nn.silu(jnp.dot(normed, up_weight, precision=high))
     slots = own_group * share + jnp.arange(share, dtype=jnp.int32)
     keep = (slots < count).astype(jnp.float32)[:, None]
-    return (residual + jnp.dot(hidden, down_weight, precision=exact)) * keep
+    return (residual + jnp.dot(hidden, down_weight, precision=high)) * keep
 
 
 def solution(mesh):

time: 145 us -> 144 us (level)
  matrix products: 12 us -> 9.79 us
  local copies, waits for them, and re-layouts: 5.31 us -> 7.08 us
    dot_general x4 -> x5, matrix products: 5.28 us -> 3.08 us  [the longest x2 1.59 us: shards(): jnp.dot(basis_part, values[part], precision=high)]
    mul x1 -> x2, other arithmetic: 6.84 us -> 7.83 us  [basis_t(): return cos_turns(turns) * live[None, slots]]
  transfers between devices with their start and end apart: 5 -> 5, of which waited for: 3 -> 3; matrix products, arithmetic and copies ran while one was open for 16% -> 17% of each run, Pallas kernels for 0% -> 0%
where the time goes in v4:
time: 144 us; the launch traced here: 142 us
  blocking collectives  47.1 us (33%)
  waiting for transfers between devices  33.7 us (23%)
  starting transfers between devices  26.3 us (18%)
  other arithmetic  17.9 us (12%)
  matrix products  9.79 us (7%)
  local copies, waits for them, and re-layouts  7.08 us (5%)
    all_to_all x3, waiting for transfers between devices, exchange(): lax.all_to_all(blocks, axes, 0, 0, axis_index_groups=sets, tiled=True)  33.7 us
    all_gather x1, blocking collectives, shards(): raw = jnp.sum(lax.all_gather(close, 'far', axis=0), axis=0)  28.8 us
    all_to_all x3, starting transfers between devices, exchange(): lax.all_to_all(blocks, axes, 0, 0, axis_index_groups=sets, tiled=True)  18.3 us
    all_gather x1, blocking collectives, shards(): t_own = lax.all_gather(mixed, 'near', axis=0, tiled=True)  18.3 us
    ppermute x2, starting transfers between devices, swap_cores(): return lax.ppermute(block, 'core', [(0, 1), (1, 0)])  7.98 us
    mul x2, other arithmetic, basis_t(): return cos_turns(turns) * live[None, slots]  7.83 us
    mul x1, other arithmetic, basis(): return cos_turns(turns) * live[:, None]  6.59 us
  transfers between devices with their start and end apart: 5, of which 3 were waited for; matrix products, arithmetic and copies ran while one was open for 17% of the time, Pallas kernels for 0%

profile of v4, /device:TPU:1, one launch (start us, length us, event | category | flops | bytes accessed | tf_op | source)
XLA Modules:
  0.0 142.3 jit_solution(16969565042790916946)
XLA Ops:
  0.0 2.3 %broadcast_in_dim.81 = f32[16,96,256]{2,1,0:T(8,128)} broadcast(f32[96,256]{1,0:T(8,128)} %param.12), dimensions={1,2} | broadcast | bytes 1671168 | tf_op jit(solution)/shard_map/broadcast_in_dim | solution.py:35
  2.3 7.6 %all-to-all-start = ((f32[16,96,256]{2,1,0:T(8,128)}), f32[16,96,256]{2,1,0:T(8,128)S(1)}, u32[]{:S(2)}, u32[]{:S(2)}) async-start(f32[16,96,256]{2,1,0:T(8,128)} %broadcast_in_dim.81), calls=%async_computation | async-start | bytes 3145728 | tf_op jit(solution)/shard_map/all_to_all | solution.py:30
  9.9 0.6 dynamic_slice.14
  10.5 0.6 fusion.40
  11.2 0.1 fusion.51
  11.2 0.1 fusion.52
  11.3 0.1 fusion.47
  11.4 0.1 fusion.48
  11.5 0.1 broadcast_in_dim.77
  11.6 0.1 reshape.120
  11.8 0.1 concatenate.39
  11.9 0.1 concatenate.33
  12.0 0.1 concatenate.37
  12.1 0.1 broadcast_in_dim.79
  12.2 0.1 reshape.121
  12.3 0.1 concatenate.40
  12.4 0.1 concatenate.34
  12.5 0.1 concatenate.38
  12.6 0.1 broadcast_in_dim.70
  12.6 0.1 add.228
  12.9 4.0 %fusion.5 = f32[512,1536]{1,0:T(8,128)} fusion(f32[1536]{0:T(1024)S(1)} %concatenate.34, f32[512]{0:T(512)S(1)} %add.228, f32[1536]{0:T(1024)S(1)} %get-tuple-element.16, f32[512]{0:T(512)S(1)} %bitcast.63, f32[1536]{0:T(1024)S(1)} %get-tuple-element.17, f32[512]{0:T(512)S(1)} %bitcast.62, f32[1536]{0:T(1024)S(1)} %get-tuple-element.15, f32[512]{0:T(512)S(1)} %bitcast.61), kind=kLoop, calls=%fused_computation.11 | loop fusion | flops 17301504 | bytes 3178496 | tf_op jit(solution)/shard_map/mul | solution.py:90
  16.9 3.8 %fusion.15 = (f32[512,768]{1,0:T(8,128)}, f32[512,768]{1,0:T(8,128)}) fusion(f32[768]{0:T(1024)S(1)} %concatenate.40, f32[768]{0:T(1024)S(1)} %get-tuple-element.19, f32[768]{0:T(1024)S(1)} %get-tuple-element.20, f32[768]{0:T(1024)S(1)} %get-tuple-element.18, f32[512]{0:T(512)S(1)} %add.228, f32[512]{0:T(512)S(1)} %bitcast.60, f32[512]{0:T(512)S(1)} %bitcast.59, ...), kind=kLoop, calls=%fused_computation.32 | loop fusion | flops 17301504 | bytes 3178496 | tf_op jit(solution)/shard_map/mul | solution.py:90
  20.7 0.1 fusion.42
  20.8 0.1 slice.296
  20.9 0.1 broadcast_in_dim.76
  21.0 0.1 slice.294
  21.1 0.1 broadcast_in_dim.74
  21.2 0.1 slice.292
  21.3 0.1 broadcast_in_dim.72
  21.4 0.1 slice.277
  21.5 0.1 broadcast_in_dim.69
  21.6 0.1 slice.274
  21.7 0.1 broadcast_in_dim.67
  21.7 0.1 slice.271
  21.8 0.1 broadcast_in_dim.65
  21.9 6.6 %fusion.3 = (f32[1536,512]{1,0:T(8,128)}, f32[1536,512]{1,0:T(8,128)}) fusion(f32[512]{0:T(512)S(1)} %broadcast_in_dim.76, f32[512]{0:T(512)S(1)} %broadcast_in_dim.74, f32[512]{0:T(512)S(1)} %broadcast_in_dim.72, f32[1536]{0:T(1024)S(1)} %concatenate.34, f32[512]{0:T(512)S(1)} %add.228, f32[1536]{0:T(1024)S(1)} %get-tuple-element.16, ...), kind=kLoop, calls=%fused_computation.9 | loop fusion | flops 34603008 | bytes 6330368 | tf_op jit(solution)/shard_map/mul | solution.py:86
  28.5 2.8 %all-to-all-done = f32[16,96,256]{2,1,0:T(8,128)S(1)} async-done(((f32[16,96,256]{2,1,0:T(8,128)}), f32[16,96,256]{2,1,0:T(8,128)S(1)}, u32[]{:S(2)}, u32[]{:S(2)}) %all-to-all-start) | async-done | bytes 1572896 | tf_op jit(solution)/shard_map/all_to_all | solution.py:30
  31.4 0.1 fusion.45
  31.5 1.3 copy-done.5
  32.8 0.8 fusion.54
  33.6 0.8 convolution_add_fusion.1
  34.4 3.8 %collective-permute-start = (f32[512,256]{1,0:T(8,128)S(1)}, f32[512,256]{1,0:T(8,128)S(1)}, u32[]{:S(2)}, u32[]{:S(2)}) collective-permute-start(f32[512,256]{1,0:T(8,128)S(1)} %convolution_add_fusion.1), channel_id=1, source_target_pairs={{0,16},{16,0},{1,17},{17,1},{2,18},{18,2},{3,19},{19,3},{4,20},{20... | collective-permute-start | bytes 1572872 | tf_op jit(solution)/shard_map/ppermute | solution.py:39
  38.3 1.4 %fusion.53 = f32[512,256]{1,0:T(8,128)S(1)} fusion(f32[512,1536]{1,0:T(8,128)S(1)} %copy-done.2, f32[1536,256]{1,0:T(8,128)S(1)} %bitcast.48), kind=kOutput, calls=%fused_computation.112 | convolution fusion | flops 1207959552 | bytes 5242880 | tf_op jit(solution)/shard_map/dot_general | solution.py:112
  39.8 0.9 add.279
  40.6 4.7 %all-to-all-start.1 = ((f32[4,128,256]{2,1,0:T(8,128)}), f32[4,128,256]{2,1,0:T(8,128)S(1)}, u32[]{:S(2)}, u32[]{:S(2)}) async-start(f32[4,128,256]{2,1,0:T(8,128)} %bitcast.10), calls=%async_computation.1 | async-start | bytes 1048576 | tf_op jit(solution)/shard_map/all_to_all | solution.py:30
  45.4 0.9 dynamic-slice_multiply_fusion
  46.3 0.4 fusion.25
  46.7 0.4 fusion.23
  47.1 10.3 %all-to-all-done.1 = f32[4,128,256]{2,1,0:T(8,128)S(1)} async-done(((f32[4,128,256]{2,1,0:T(8,128)}), f32[4,128,256]{2,1,0:T(8,128)S(1)}, u32[]{:S(2)}, u32[]{:S(2)}) %all-to-all-start.1) | async-done | bytes 524320 | tf_op jit(solution)/shard_map/all_to_all | solution.py:30
  57.4 28.8 %all-gather = f32[512,256]{1,0:T(8,128)S(1)} all-gather(f32[128,256]{1,0:T(8,128)S(1)} %reduce_sum.36), channel_id=2, replica_groups=mesh['far'=4,'near'=4,'core'=2,'kvec'=16] {'far'}, dimensions={0}, use_global_device_ids=true | all-gather | bytes 655360 | tf_op jit(solution)/shard_map/all_gather | solution.py:114
  86.3 0.2 fusion.21
  86.6 0.2 fusion.55
  86.9 0.2 convolution_add_fusion.2
  87.1 18.3 %all_gather.11 = f32[512,256]{1,0:T(8,128)S(1)} all-gather(f32[128,256]{1,0:T(8,128)S(1)} %convolution_add_fusion.2), channel_id=1, replica_groups=mesh['far'=4,'near'=4,'core'=2,'kvec'=16] {'near'}, dimensions={0}, use_global_device_ids=true | all-gather | bytes 655360 | tf_op jit(solution)/shard_map/all_gather | solution.py:126
  105.4 4.1 %collective-permute-start.1 = (f32[512,256]{1,0:T(8,128)S(1)}, f32[512,256]{1,0:T(8,128)S(1)}, u32[]{:S(2)}, u32[]{:S(2)}) collective-permute-start(f32[512,256]{1,0:T(8,128)S(1)} %all_gather.11), channel_id=1, source_target_pairs={{0,16},{16,0},{1,17},{17,1},{2,18},{18,2},{3,19},{19,3},{4,20},{20... | collective-permute-start | bytes 1572872 | tf_op jit(solution)/shard_map/ppermute | solution.py:39
  109.5 1.5 %fusion.56 = f32[1536,256]{1,0:T(8,128)S(1)} fusion(f32[1536,512]{1,0:T(8,128)S(1)} %copy-done.1, f32[512,256]{1,0:T(8,128)S(1)} %all_gather.11), kind=kOutput, calls=%fused_computation.115 | convolution fusion | flops 1207959552 | bytes 5242880 | tf_op jit(solution)/shard_map/dot_general | solution.py:128
  111.0 2.6 %convolution_add_fusion = f32[1536,256]{1,0:T(8,128)} fusion(f32[1536,256]{1,0:T(8,128)S(1)} %fusion.56, f32[1536,512]{1,0:T(8,128)S(1)} %copy-done.3, f32[512,256]{1,0:T(8,128)S(1)} %collective-permute-done.1), kind=kOutput, calls=%fused_computation.24 | convolution fusion | flops 1208352768 | bytes 6815744 | tf_op jit(solution)/shard_map/dot_general | solution.py:128
  113.6 6.0 %all-to-all-start.2 = ((f32[16,96,256]{2,1,0:T(8,128)}), f32[16,96,256]{2,1,0:T(8,128)S(1)}, u32[]{:S(2)}, u32[]{:S(2)}) async-start(f32[16,96,256]{2,1,0:T(8,128)} %bitcast.49), calls=%async_computation.2 | async-start | bytes 3145728 | tf_op jit(solution)/shard_map/all_to_all | solution.py:30
  119.6 0.7 compare_convert_fusion
  120.3 20.5 %all-to-all-done.2 = f32[16,96,256]{2,1,0:T(8,128)S(1)} async-done(((f32[16,96,256]{2,1,0:T(8,128)}), f32[16,96,256]{2,1,0:T(8,128)S(1)}, u32[]{:S(2)}, u32[]{:S(2)}) %all-to-all-start.2) | async-done | bytes 1572896 | tf_op jit(solution)/shard_map/all_to_all | solution.py:30
  140.8 0.1 reduce_sum.38
  140.9 0.1 multiply_reduce_fusion
  141.0 0.3 fusion.35
  141.4 0.9 fusion.20
  (58 shorter events, 0.5 us)
Async XLA Ops:
  0.0 141.0 %copy-start = (f32[256,512]{1,0:T(8,128)S(1)}, f32[256,512]{1,0:T(8,128)}, u32[]{:S(2)}) copy-start(f32[256,512]{1,0:T(8,128)} %param.21) | copy-start | bytes 1572868
  0.0 12.6 %copy-start.13 = (f32[2]{0:T(128)S(1)}, f32[2]{0:T(128)}, u32[]{:S(2)}) copy-start(f32[2]{0:T(128)} %constant.24.clone) | copy-start | bytes 28
  0.0 9.9 %copy-start.15 = (s32[32]{0:T(128)S(1)}, s32[32]{0:T(128)}, u32[]{:S(2)}) copy-start(s32[32]{0:T(128)} %param.15) | copy-start | bytes 388
  0.0 11.3 %copy-start.10 = (s32[3,1536]{1,0:T(4,128)S(1)}, s32[3,1536]{1,0:T(4,128)}, u32[]{:S(2)}) copy-start(s32[3,1536]{1,0:T(4,128)} %param.13) | copy-start | bytes 55300
  0.0 11.5 %copy-start.11 = (s32[3,512]{1,0:T(4,128)S(1)}, s32[3,512]{1,0:T(4,128)}, u32[]{:S(2)}) copy-start(s32[3,512]{1,0:T(4,128)} %param.14) | copy-start | bytes 18436
  2.3 29.1 %all-to-all-start = ((f32[16,96,256]{2,1,0:T(8,128)}), f32[16,96,256]{2,1,0:T(8,128)S(1)}, u32[]{:S(2)}, u32[]{:S(2)}) async-start(f32[16,96,256]{2,1,0:T(8,128)} %broadcast_in_dim.81), calls=%async_computation | async-start | bytes 3145728 | tf_op jit(solution)/shard_map/all_to_all | solution.py:30
  31.4 1.4 copy-start.5
  31.4 2.2 %copy-start.4 = (f32[512,768]{1,0:T(8,128)S(1)}, f32[512,768]{1,0:T(8,128)}, u32[]{:S(2)}) copy-start(f32[512,768]{1,0:T(8,128)} %get-tuple-element.13) | copy-start | bytes 4718596
  32.8 5.5 %copy-start.2 = (f32[512,1536]{1,0:T(8,128)S(1)}, f32[512,1536]{1,0:T(8,128)}, u32[]{:S(2)}) copy-start(f32[512,1536]{1,0:T(8,128)} %fusion.5) | copy-start | bytes 9437188
  34.4 5.4 %collective-permute-start = (f32[512,256]{1,0:T(8,128)S(1)}, f32[512,256]{1,0:T(8,128)S(1)}, u32[]{:S(2)}, u32[]{:S(2)}) collective-permute-start(f32[512,256]{1,0:T(8,128)S(1)} %convolution_add_fusion.1), channel_id=1, source_target_pairs={{0,16},{16,0},{1,17},{17,1},{2,18},{18,2},{3,19},{19,3},{4,20},{20... | collective-permute-start | bytes 1572872 | tf_op jit(solution)/shard_map/ppermute | solution.py:39
  38.3 8.0 %copy-start.6 = (f32[256,256]{1,0:T(8,128)S(1)}, f32[256,256]{1,0:T(8,128)}, u32[]{:S(2)}) copy-start(f32[256,256]{1,0:T(8,128)} %param.19) | copy-start | bytes 786436
  38.3 8.0 %copy-start.7 = (f32[2,256,256]{2,1,0:T(8,128)S(1)}, f32[2,256,256]{2,1,0:T(8,128)}, u32[]{:S(2)}) copy-start(f32[2,256,256]{2,1,0:T(8,128)} %param.18) | copy-start | bytes 1572868
  39.7 46.6 %copy-start.9 = (f32[256,256]{1,0:T(8,128)S(1)}, f32[256,256]{1,0:T(8,128)}, u32[]{:S(2)}) copy-start(f32[256,256]{1,0:T(8,128)} %param.16) | copy-start | bytes 786436
  40.6 16.8 %all-to-all-start.1 = ((f32[4,128,256]{2,1,0:T(8,128)}), f32[4,128,256]{2,1,0:T(8,128)S(1)}, u32[]{:S(2)}, u32[]{:S(2)}) async-start(f32[4,128,256]{2,1,0:T(8,128)} %bitcast.10), calls=%async_computation.1 | async-start | bytes 1048576 | tf_op jit(solution)/shard_map/all_to_all | solution.py:30
  86.3 23.2 %copy-start.1 = (f32[1536,512]{1,0:T(8,128)S(1)}, f32[1536,512]{1,0:T(8,128)}, u32[]{:S(2)}) copy-start(f32[1536,512]{1,0:T(8,128)} %get-tuple-element.10) | copy-start | bytes 9437188
  86.9 24.1 %copy-start.3 = (f32[1536,512]{1,0:T(8,128)S(1)}, f32[1536,512]{1,0:T(8,128)}, u32[]{:S(2)}) copy-start(f32[1536,512]{1,0:T(8,128)} %get-tuple-element.14) | copy-start | bytes 9437188
  105.4 5.6 %collective-permute-start.1 = (f32[512,256]{1,0:T(8,128)S(1)}, f32[512,256]{1,0:T(8,128)S(1)}, u32[]{:S(2)}, u32[]{:S(2)}) collective-permute-start(f32[512,256]{1,0:T(8,128)S(1)} %all_gather.11), channel_id=1, source_target_pairs={{0,16},{16,0},{1,17},{17,1},{2,18},{18,2},{3,19},{19,3},{4,20},{20... | collective-permute-start | bytes 1572872 | tf_op jit(solution)/shard_map/ppermute | solution.py:39
  113.6 27.3 %copy-start.8 = (f32[96,256]{1,0:T(8,128)S(1)}, f32[96,256]{1,0:T(8,128)}, u32[]{:S(2)}) copy-start(f32[96,256]{1,0:T(8,128)} %param.12) | copy-start | bytes 294916
  113.6 27.4 %copy-start.12 = (f32[256]{0:T(256)S(1)}, f32[256]{0:T(256)}, u32[]{:S(2)}) copy-start(f32[256]{0:T(256)} %param.20) | copy-start | bytes 3076
  113.6 27.7 %copy-start.14 = (f32[512,256]{1,0:T(8,128)S(1)}, f32[512,256]{1,0:T(8,128)}, u32[]{:S(2)}) copy-start(f32[512,256]{1,0:T(8,128)} %param.22) | copy-start | bytes 1572868
  113.6 27.2 %all-to-all-start.2 = ((f32[16,96,256]{2,1,0:T(8,128)}), f32[16,96,256]{2,1,0:T(8,128)S(1)}, u32[]{:S(2)}, u32[]{:S(2)}) async-start(f32[16,96,256]{2,1,0:T(8,128)} %bitcast.49), calls=%async_computation.2 | async-start | bytes 3145728 | tf_op jit(solution)/shard_map/all_to_all | solution.py:30

commit v5 on v4

--- a/solution.py
+++ b/solution.py
@@ -94,10 +94,8 @@
 
     w_own, w_other = lines(core), lines(1 - core)
     parts = [slice(0, capacity // 2), slice(capacity // 2, capacity)]
-    own, other, own_t, other_t = lax.optimization_barrier(
+    own_t, other_t = lax.optimization_barrier(
         (
-            basis(w_own),
-            basis(w_other),
             basis_t(looped(w_own), slice(0, capacity)),
             [basis_t(looped(w_other), part) for part in parts],
         )
@@ -110,7 +108,9 @@
         sum(jnp.dot(basis_part, values[part], precision=high) for basis_part, part in zip(other_t, parts))
     )
     summed = lax.optimization_barrier(jnp.dot(own_t, values, precision=high)) + passed
+    summed, w_own, w_other = lax.optimization_barrier((summed, w_own, w_other))
     close = jnp.sum(exchange(summed.reshape(near, far * rows, width), "near", LOOP), axis=0)
+    close, own, other = lax.optimization_barrier((close, basis(w_own), basis(w_other)))
     raw = jnp.sum(lax.all_gather(close, "far", axis=0), axis=0)
     total = jnp.dot(raw, value_weight, precision=high).reshape(far, 2, k_own, width)
     real_sf, imag_sf = total[:, 0], total[:, 1]

time: 144 us -> 143 us (level)
    all_gather x1, blocking collectives: 18.3 us -> 16.7 us  [shards(): t_own = lax.all_gather(mixed, 'near', axis=0, tiled=True)]
  transfers between devices with their start and end apart: 5 -> 5, of which waited for: 3 -> 3; matrix products, arithmetic and copies ran while one was open for 17% -> 16% of each run, Pallas kernels for 0% -> 0%
where the time goes in v5:
time: 143 us; the launch traced here: 142 us
  blocking collectives  46.4 us (32%)
  waiting for transfers between devices  34.6 us (24%)
  starting transfers between devices  26.3 us (18%)
  other arithmetic  17.7 us (12%)
  matrix products  9.72 us (7%)
  local copies, waits for them, and re-layouts  6.28 us (4%)
    all_to_all x3, waiting for transfers between devices, exchange(): lax.all_to_all(blocks, axes, 0, 0, axis_index_groups=sets, tiled=True)  34.6 us
    all_gather x1, blocking collectives, shards(): raw = jnp.sum(lax.all_gather(close, 'far', axis=0), axis=0)  29.7 us
    all_to_all x3, starting transfers between devices, exchange(): lax.all_to_all(blocks, axes, 0, 0, axis_index_groups=sets, tiled=True)  18.3 us
    all_gather x1, blocking collectives, shards(): t_own = lax.all_gather(mixed, 'near', axis=0, tiled=True)  16.7 us
    ppermute x2, starting transfers between devices, swap_cores(): return lax.ppermute(block, 'core', [(0, 1), (1, 0)])  7.96 us
    mul x2, other arithmetic, basis_t(): return cos_turns(turns) * live[None, slots]  7.69 us
    mul x1, other arithmetic, basis(): return cos_turns(turns) * live[:, None]  6.59 us
  transfers between devices with their start and end apart: 5, of which 3 were waited for; matrix products, arithmetic and copies ran while one was open for 16% of the time, Pallas kernels for 0%

profile of v5, /device:TPU:1, one launch (start us, length us, event | category | flops | bytes accessed | tf_op | source)
XLA Modules:
  0.0 141.6 jit_solution(13274976796549614632)
XLA Ops:
  0.0 0.0 copy-start
  0.0 0.0 copy-start.20
  0.0 0.0 copy-start.21
  0.0 2.2 %broadcast_in_dim.17 = f32[16,96,256]{2,1,0:T(8,128)} broadcast(f32[96,256]{1,0:T(8,128)} %param.12), dimensions={1,2} | broadcast | bytes 1671168 | tf_op jit(solution)/shard_map/broadcast_in_dim | solution.py:35
  2.3 7.6 %all-to-all-start = ((f32[16,96,256]{2,1,0:T(8,128)}), f32[16,96,256]{2,1,0:T(8,128)S(1)}, u32[]{:S(2)}, u32[]{:S(2)}) async-start(f32[16,96,256]{2,1,0:T(8,128)} %broadcast_in_dim.17), calls=%async_computation | async-start | bytes 3145728 | tf_op jit(solution)/shard_map/all_to_all | solution.py:30
  9.9 0.0 copy-done.25
  9.9 0.6 dynamic_slice.14
  10.5 0.6 fusion.40
  11.1 0.1 fusion.51
  11.2 0.1 fusion.52
  11.3 0.1 fusion.45
  11.4 0.1 fusion.46
  11.5 0.1 broadcast_in_dim.12
  11.6 0.1 reshape.84
  11.7 0.1 concatenate.39
  11.8 0.1 concatenate.34
  11.9 0.1 concatenate.37
  12.0 0.3 copy-done.14
  12.3 0.1 broadcast_in_dim.15
  12.4 0.1 reshape.85
  12.6 0.1 concatenate.40
  12.6 0.1 concatenate.35
  12.7 0.1 concatenate.38
  12.8 0.0 copy-done.23
  12.8 0.1 broadcast_in_dim.14
  12.9 0.1 add.228
  13.0 0.1 slice_reduce_fusion.5
  13.1 0.1 copy-done.16
  13.1 3.8 %fusion.15 = (f32[512,768]{1,0:T(8,128)}, f32[512,768]{1,0:T(8,128)}) fusion(f32[768]{0:T(1024)S(1)} %concatenate.40, f32[768]{0:T(1024)S(1)} %get-tuple-element.27, f32[768]{0:T(1024)S(1)} %get-tuple-element.28, f32[768]{0:T(1024)S(1)} %get-tuple-element.26, f32[512]{0:T(512)S(1)} %add.228, f32[512]{0:T(512)S(1)} %bitcast.72, f32[512]{0:T(512)S(1)} %bitcast.71, ...), kind=kLoop, calls=%fused_computation.32 | loop fusion | flops 17301504 | bytes 3178496 | tf_op jit(solution)/shard_map/mul | solution.py:90
  17.0 0.1 slice_reduce_fusion.2
  17.0 3.9 %fusion.1 = f32[512,1536]{1,0:T(8,128)} fusion(f32[1536]{0:T(1024)S(1)} %concatenate.35, f32[512]{0:T(512)S(1)} %add.228, f32[1536]{0:T(1024)S(1)} %get-tuple-element.24, f32[512]{0:T(512)S(1)} %bitcast.75, f32[1536]{0:T(1024)S(1)} %get-tuple-element.25, f32[512]{0:T(512)S(1)} %bitcast.74, f32[1536]{0:T(1024)S(1)} %get-tuple-element.23, f32[512]{0:T(512)S(1)} %bitcast.73), kind=kLoop, calls=%fused_computation.7 | loop fusion | flops 17301504 | bytes 3178496 | tf_op jit(solution)/shard_map/mul | solution.py:90
  20.9 0.9 dynamic-slice_multiply_fusion
  21.9 0.4 fusion.25
  22.3 0.4 fusion.23
  22.7 8.7 %all-to-all-done = f32[16,96,256]{2,1,0:T(8,128)S(1)} async-done(((f32[16,96,256]{2,1,0:T(8,128)}), f32[16,96,256]{2,1,0:T(8,128)S(1)}, u32[]{:S(2)}, u32[]{:S(2)}) %all-to-all-start) | async-done | bytes 1572896 | tf_op jit(solution)/shard_map/all_to_all | solution.py:30
  31.3 0.1 fusion.43
  31.5 1.3 copy-done.5
  32.8 0.8 fusion.54
  33.6 0.8 convolution_add_fusion.1
  34.4 3.9 %collective-permute-start = (f32[512,256]{1,0:T(8,128)S(1)}, f32[512,256]{1,0:T(8,128)S(1)}, u32[]{:S(2)}, u32[]{:S(2)}) collective-permute-start(f32[512,256]{1,0:T(8,128)S(1)} %convolution_add_fusion.1), channel_id=1, source_target_pairs={{0,16},{16,0},{1,17},{17,1},{2,18},{18,2},{3,19},{19,3},{4,20},{20... | collective-permute-start | bytes 1572872 | tf_op jit(solution)/shard_map/ppermute | solution.py:39
  38.3 0.0 copy-start.17
  38.3 1.4 %fusion.53 = f32[512,256]{1,0:T(8,128)S(1)} fusion(f32[512,1536]{1,0:T(8,128)S(1)} %copy-done.2, f32[1536,256]{1,0:T(8,128)S(1)} %bitcast.54), kind=kOutput, calls=%fused_computation.106 | convolution fusion | flops 1207959552 | bytes 5242880 | tf_op jit(solution)/shard_map/dot_general | solution.py:110
  39.8 0.0 collective-permute-done
  39.8 0.9 add.262
  40.6 4.7 %all-to-all-start.1 = ((f32[4,128,256]{2,1,0:T(8,128)}), f32[4,128,256]{2,1,0:T(8,128)S(1)}, u32[]{:S(2)}, u32[]{:S(2)}) async-start(f32[4,128,256]{2,1,0:T(8,128)} %bitcast.10), calls=%async_computation.1 | async-start | bytes 1048576 | tf_op jit(solution)/shard_map/all_to_all | solution.py:30
  45.4 0.0 copy-start.9
  45.4 6.6 %fusion.5 = (f32[1536,512]{1,0:T(8,128)}, f32[1536,512]{1,0:T(8,128)}) fusion(f32[512]{0:T(512)S(1)} %bitcast.65, f32[512]{0:T(512)S(1)} %bitcast.66, f32[512]{0:T(512)S(1)} %bitcast.64, f32[1536]{0:T(1024)S(1)} %concatenate.35, f32[512]{0:T(512)S(1)} %copy-done.19, f32[1536]{0:T(1024)S(1)} %copy-done.11, f32[1536]{0:T(1024)S(1)} %copy-done.13, ...), kind=kLoop, calls=%fused_computation.11 | loop fusion | flops 34603008 | bytes 6330368 | tf_op jit(solution)/shard_map/mul | solution.py:86
  52.0 5.4 %all-to-all-done.1 = f32[4,128,256]{2,1,0:T(8,128)S(1)} async-done(((f32[4,128,256]{2,1,0:T(8,128)}), f32[4,128,256]{2,1,0:T(8,128)S(1)}, u32[]{:S(2)}, u32[]{:S(2)}) %all-to-all-start.1) | async-done | bytes 524320 | tf_op jit(solution)/shard_map/all_to_all | solution.py:30
  57.5 29.7 %all-gather = f32[512,256]{1,0:T(8,128)S(1)} all-gather(f32[128,256]{1,0:T(8,128)S(1)} %reduce_sum.36), channel_id=2, replica_groups=mesh['far'=4,'near'=4,'core'=2,'kvec'=16] {'far'}, dimensions={0}, use_global_device_ids=true | all-gather | bytes 655360 | tf_op jit(solution)/shard_map/all_gather | solution.py:114
  87.3 0.2 fusion.21
  87.6 0.2 fusion.55
  87.8 0.2 convolution_add_fusion.2
  88.1 16.7 %all_gather.11 = f32[512,256]{1,0:T(8,128)S(1)} all-gather(f32[128,256]{1,0:T(8,128)S(1)} %convolution_add_fusion.2), channel_id=1, replica_groups=mesh['far'=4,'near'=4,'core'=2,'kvec'=16] {'near'}, dimensions={0}, use_global_device_ids=true | all-gather | bytes 655360 | tf_op jit(solution)/shard_map/all_gather | solution.py:126
  104.8 4.1 %collective-permute-start.1 = (f32[512,256]{1,0:T(8,128)S(1)}, f32[512,256]{1,0:T(8,128)S(1)}, u32[]{:S(2)}, u32[]{:S(2)}) collective-permute-start(f32[512,256]{1,0:T(8,128)S(1)} %all_gather.11), channel_id=1, source_target_pairs={{0,16},{16,0},{1,17},{17,1},{2,18},{18,2},{3,19},{19,3},{4,20},{20... | collective-permute-start | bytes 1572872 | tf_op jit(solution)/shard_map/ppermute | solution.py:39
  108.9 1.4 fusion.56
  110.3 0.0 collective-permute-done.1
  110.3 2.6 %convolution_add_fusion = f32[1536,256]{1,0:T(8,128)} fusion(f32[1536,256]{1,0:T(8,128)S(1)} %fusion.56, f32[1536,512]{1,0:T(8,128)S(1)} %copy-done.3, f32[512,256]{1,0:T(8,128)S(1)} %collective-permute-done.1), kind=kOutput, calls=%fused_computation.24 | convolution fusion | flops 1208352768 | bytes 6815744 | tf_op jit(solution)/shard_map/dot_general | solution.py:128
  112.9 6.0 %all-to-all-start.2 = ((f32[16,96,256]{2,1,0:T(8,128)}), f32[16,96,256]{2,1,0:T(8,128)S(1)}, u32[]{:S(2)}, u32[]{:S(2)}) async-start(f32[16,96,256]{2,1,0:T(8,128)} %bitcast.55), calls=%async_computation.2 | async-start | bytes 3145728 | tf_op jit(solution)/shard_map/all_to_all | solution.py:30
  118.9 0.6 compare_convert_fusion
  119.6 20.5 %all-to-all-done.2 = f32[16,96,256]{2,1,0:T(8,128)S(1)} async-done(((f32[16,96,256]{2,1,0:T(8,128)}), f32[16,96,256]{2,1,0:T(8,128)S(1)}, u32[]{:S(2)}, u32[]{:S(2)}) %all-to-all-start.2) | async-done | bytes 1572896 | tf_op jit(solution)/shard_map/all_to_all | solution.py:30
  140.1 0.1 reduce_sum.38
  140.2 0.1 multiply_reduce_fusion
  140.3 0.3 fusion.35
  140.6 0.9 fusion.20
  (61 shorter events, 0.3 us)
Async XLA Ops:
  0.0 140.3 %copy-start = (f32[256,512]{1,0:T(8,128)S(1)}, f32[256,512]{1,0:T(8,128)}, u32[]{:S(2)}) copy-start(f32[256,512]{1,0:T(8,128)} %param.21) | copy-start | bytes 1572868
  0.0 12.8 %copy-start.23 = (f32[2]{0:T(128)S(1)}, f32[2]{0:T(128)}, u32[]{:S(2)}) copy-start(f32[2]{0:T(128)} %constant.24.clone) | copy-start | bytes 28
  0.0 9.9 %copy-start.25 = (s32[32]{0:T(128)S(1)}, s32[32]{0:T(128)}, u32[]{:S(2)}) copy-start(s32[32]{0:T(128)} %param.15) | copy-start | bytes 388
  0.0 11.3 %copy-start.20 = (s32[3,1536]{1,0:T(4,128)S(1)}, s32[3,1536]{1,0:T(4,128)}, u32[]{:S(2)}) copy-start(s32[3,1536]{1,0:T(4,128)} %param.13) | copy-start | bytes 55300
  0.0 11.4 %copy-start.21 = (s32[3,512]{1,0:T(4,128)S(1)}, s32[3,512]{1,0:T(4,128)}, u32[]{:S(2)}) copy-start(s32[3,512]{1,0:T(4,128)} %param.14) | copy-start | bytes 18436
  2.3 29.1 %all-to-all-start = ((f32[16,96,256]{2,1,0:T(8,128)}), f32[16,96,256]{2,1,0:T(8,128)S(1)}, u32[]{:S(2)}, u32[]{:S(2)}) async-start(f32[16,96,256]{2,1,0:T(8,128)} %broadcast_in_dim.17), calls=%async_computation | async-start | bytes 3145728 | tf_op jit(solution)/shard_map/all_to_all | solution.py:30
  11.7 0.6 copy-start.14
  12.5 0.6 copy-start.16
  13.0 8.0 %copy-start.18 = (f32[512]{0:T(512)}, f32[512]{0:T(512)S(1)}, u32[]{:S(2)}) copy-start(f32[512]{0:T(512)S(1)} %add.228) | copy-start | bytes 6148
  13.1 8.7 %copy-start.6 = (f32[256,256]{1,0:T(8,128)S(1)}, f32[256,256]{1,0:T(8,128)}, u32[]{:S(2)}) copy-start(f32[256,256]{1,0:T(8,128)} %param.19) | copy-start | bytes 786436
  13.1 8.7 %copy-start.7 = (f32[2,256,256]{2,1,0:T(8,128)S(1)}, f32[2,256,256]{2,1,0:T(8,128)}, u32[]{:S(2)}) copy-start(f32[2,256,256]{2,1,0:T(8,128)} %param.18) | copy-start | bytes 1572868
  17.0 3.9 %copy-start.10 = (f32[1536]{0:T(1024)}, f32[1536]{0:T(1024)S(1)}, u32[]{:S(2)}) copy-start(f32[1536]{0:T(1024)S(1)} %get-tuple-element.24) | copy-start | bytes 18436
  17.0 3.9 %copy-start.12 = (f32[1536]{0:T(1024)}, f32[1536]{0:T(1024)S(1)}, u32[]{:S(2)}) copy-start(f32[1536]{0:T(1024)S(1)} %get-tuple-element.25) | copy-start | bytes 18436
  31.3 1.4 copy-start.5
  31.3 2.2 %copy-start.4 = (f32[512,768]{1,0:T(8,128)S(1)}, f32[512,768]{1,0:T(8,128)}, u32[]{:S(2)}) copy-start(f32[512,768]{1,0:T(8,128)} %get-tuple-element.16) | copy-start | bytes 4718596
  32.8 5.5 %copy-start.2 = (f32[512,1536]{1,0:T(8,128)S(1)}, f32[512,1536]{1,0:T(8,128)}, u32[]{:S(2)}) copy-start(f32[512,1536]{1,0:T(8,128)} %fusion.1) | copy-start | bytes 9437188
  34.4 5.4 %collective-permute-start = (f32[512,256]{1,0:T(8,128)S(1)}, f32[512,256]{1,0:T(8,128)S(1)}, u32[]{:S(2)}, u32[]{:S(2)}) collective-permute-start(f32[512,256]{1,0:T(8,128)S(1)} %convolution_add_fusion.1), channel_id=1, source_target_pairs={{0,16},{16,0},{1,17},{17,1},{2,18},{18,2},{3,19},{19,3},{4,20},{20... | collective-permute-start | bytes 1572872 | tf_op jit(solution)/shard_map/ppermute | solution.py:39
  38.3 7.1 %copy-start.17 = (f32[3,512]{1,0:T(4,128)S(1)}, f32[3,512]{1,0:T(4,128)}, u32[]{:S(2)}) copy-start(f32[3,512]{1,0:T(4,128)} %copy-done.16) | copy-start | bytes 18436
  38.3 7.1 %copy-start.15 = (f32[3,512]{1,0:T(4,128)S(1)}, f32[3,512]{1,0:T(4,128)}, u32[]{:S(2)}) copy-start(f32[3,512]{1,0:T(4,128)} %copy-done.14) | copy-start | bytes 18436
  38.3 7.1 %copy-start.11 = (f32[1536]{0:T(1024)S(1)}, f32[1536]{0:T(1024)}, u32[]{:S(2)}) copy-start(f32[1536]{0:T(1024)} %copy-done.10) | copy-start | bytes 18436
  38.3 7.1 %copy-start.13 = (f32[1536]{0:T(1024)S(1)}, f32[1536]{0:T(1024)}, u32[]{:S(2)}) copy-start(f32[1536]{0:T(1024)} %copy-done.12) | copy-start | bytes 18436
  38.3 7.1 %copy-start.19 = (f32[512]{0:T(512)S(1)}, f32[512]{0:T(512)}, u32[]{:S(2)}) copy-start(f32[512]{0:T(512)} %copy-done.18) | copy-start | bytes 6148
  40.6 16.8 %all-to-all-start.1 = ((f32[4,128,256]{2,1,0:T(8,128)}), f32[4,128,256]{2,1,0:T(8,128)S(1)}, u32[]{:S(2)}, u32[]{:S(2)}) async-start(f32[4,128,256]{2,1,0:T(8,128)} %bitcast.10), calls=%async_computation.1 | async-start | bytes 1048576 | tf_op jit(solution)/shard_map/all_to_all | solution.py:30
  45.4 41.8 %copy-start.9 = (f32[256,256]{1,0:T(8,128)S(1)}, f32[256,256]{1,0:T(8,128)}, u32[]{:S(2)}) copy-start(f32[256,256]{1,0:T(8,128)} %param.16) | copy-start | bytes 786436
  87.3 21.6 %copy-start.1 = (f32[1536,512]{1,0:T(8,128)S(1)}, f32[1536,512]{1,0:T(8,128)}, u32[]{:S(2)}) copy-start(f32[1536,512]{1,0:T(8,128)} %get-tuple-element.20) | copy-start | bytes 9437188
  87.8 22.5 %copy-start.3 = (f32[1536,512]{1,0:T(8,128)S(1)}, f32[1536,512]{1,0:T(8,128)}, u32[]{:S(2)}) copy-start(f32[1536,512]{1,0:T(8,128)} %get-tuple-element.22) | copy-start | bytes 9437188
  104.8 5.5 %collective-permute-start.1 = (f32[512,256]{1,0:T(8,128)S(1)}, f32[512,256]{1,0:T(8,128)S(1)}, u32[]{:S(2)}, u32[]{:S(2)}) collective-permute-start(f32[512,256]{1,0:T(8,128)S(1)} %all_gather.11), channel_id=1, source_target_pairs={{0,16},{16,0},{1,17},{17,1},{2,18},{18,2},{3,19},{19,3},{4,20},{20... | collective-permute-start | bytes 1572872 | tf_op jit(solution)/shard_map/ppermute | solution.py:39
  112.9 27.3 %copy-start.8 = (f32[96,256]{1,0:T(8,128)S(1)}, f32[96,256]{1,0:T(8,128)}, u32[]{:S(2)}) copy-start(f32[96,256]{1,0:T(8,128)} %param.12) | copy-start | bytes 294916
  112.9 27.4 %copy-start.22 = (f32[256]{0:T(256)S(1)}, f32[256]{0:T(256)}, u32[]{:S(2)}) copy-start(f32[256]{0:T(256)} %param.20) | copy-start | bytes 3076
  112.9 27.7 %copy-start.24 = (f32[512,256]{1,0:T(8,128)S(1)}, f32[512,256]{1,0:T(8,128)}, u32[]{:S(2)}) copy-start(f32[512,256]{1,0:T(8,128)} %param.22) | copy-start | bytes 1572868
  112.9 27.2 %all-to-all-start.2 = ((f32[16,96,256]{2,1,0:T(8,128)}), f32[16,96,256]{2,1,0:T(8,128)S(1)}, u32[]{:S(2)}, u32[]{:S(2)}) async-start(f32[16,96,256]{2,1,0:T(8,128)} %bitcast.55), calls=%async_computation.2 | async-start | bytes 3145728 | tf_op jit(solution)/shard_map/all_to_all | solution.py:30

commit v6 on v5

--- a/solution.py
+++ b/solution.py
@@ -93,7 +93,7 @@
         return jnp.concatenate([jnp.split(w, near, axis=1)[n] for n in LOOP[0]], axis=1)
 
     w_own, w_other = lines(core), lines(1 - core)
-    parts = [slice(0, capacity // 2), slice(capacity // 2, capacity)]
+    parts = [slice(0, capacity // 3), slice(capacity // 3, capacity)]
     own_t, other_t = lax.optimization_barrier(
         (
             basis_t(looped(w_own), slice(0, capacity)),

time: 143 us -> 149 us (1.042)
  matrix products: 9.72 us -> 13.2 us
  waiting for transfers between devices: 34.6 us -> 31.6 us
  local copies, waits for them, and re-layouts: 6.28 us -> 8.2 us
  starting transfers between devices: 26.3 us -> 28.2 us
  other arithmetic: 17.7 us -> 19.4 us
    all_to_all x3, waiting for transfers between devices: 34.6 us -> 31.6 us  [exchange(): lax.all_to_all(blocks, axes, 0, 0, axis_index_groups=sets, tiled=True)]
    ppermute x2, starting transfers between devices: 7.96 us -> 9.94 us  [swap_cores(): return lax.ppermute(block, 'core', [(0, 1), (1, 0)])]
    dot_general x1, matrix products: 1.44 us -> 3.31 us  [shards(): jnp.dot(own_t, values, precision=high)]
    mul x2 -> x3, other arithmetic: 7.69 us -> 8.21 us  [basis_t(): return cos_turns(turns) * live[None, slots]]
  transfers between devices with their start and end apart: 5 -> 5, of which waited for: 3 -> 3; matrix products, arithmetic and copies ran while one was open for 16% -> 20% of each run, Pallas kernels for 0% -> 0%
where the time goes in v6:
time: 149 us; the launch traced here: 148 us
  blocking collectives  46.5 us (31%)
  waiting for transfers between devices  31.6 us (21%)
  starting transfers between devices  28.2 us (19%)
  other arithmetic  19.4 us (13%)
  matrix products  13.2 us (9%)
  local copies, waits for them, and re-layouts  8.2 us (6%)
    all_to_all x3, waiting for transfers between devices, exchange(): lax.all_to_all(blocks, axes, 0, 0, axis_index_groups=sets, tiled=True)  31.6 us
    all_gather x1, blocking collectives, shards(): raw = jnp.sum(lax.all_gather(close, 'far', axis=0), axis=0)  29.2 us
    all_to_all x3, starting transfers between devices, exchange(): lax.all_to_all(blocks, axes, 0, 0, axis_index_groups=sets, tiled=True)  18.3 us
    all_gather x1, blocking collectives, shards(): t_own = lax.all_gather(mixed, 'near', axis=0, tiled=True)  17.3 us
    ppermute x2, starting transfers between devices, swap_cores(): return lax.ppermute(block, 'core', [(0, 1), (1, 0)])  9.94 us
    mul x3, other arithmetic, basis_t(): return cos_turns(turns) * live[None, slots]  8.21 us
    mul x1, other arithmetic, basis(): return cos_turns(turns) * live[:, None]  6.58 us
    dot_general x1, matrix products, shards(): jnp.dot(own_t, values, precision=high)  3.31 us
  transfers between devices with their start and end apart: 5, of which 3 were waited for; matrix products, arithmetic and copies ran while one was open for 20% of the time, Pallas kernels for 0%

profile of v6, /device:TPU:1, one launch (start us, length us, event | category | flops | bytes accessed | tf_op | source)
XLA Modules:
  0.0 147.7 jit_solution(5504391714696538666)
XLA Ops:
  0.0 2.3 %broadcast_in_dim.17 = f32[16,96,256]{2,1,0:T(8,128)} broadcast(f32[96,256]{1,0:T(8,128)} %param.12), dimensions={1,2} | broadcast | bytes 1671168 | tf_op jit(solution)/shard_map/broadcast_in_dim | solution.py:35
  2.3 7.6 %all-to-all-start = ((f32[16,96,256]{2,1,0:T(8,128)}), f32[16,96,256]{2,1,0:T(8,128)S(1)}, u32[]{:S(2)}, u32[]{:S(2)}) async-start(f32[16,96,256]{2,1,0:T(8,128)} %broadcast_in_dim.17), calls=%async_computation | async-start | bytes 3145728 | tf_op jit(solution)/shard_map/all_to_all | solution.py:30
  9.9 0.6 dynamic_slice.14
  10.5 0.5 fusion.43
  11.0 0.1 fusion.56
  11.1 0.7 fusion.55
  11.8 0.0 copy-done.10
  11.8 0.1 fusion.48
  11.9 0.1 fusion.47
  12.0 0.1 broadcast_in_dim.15
  12.1 0.1 reshape.83
  12.3 0.1 broadcast_in_dim.12
  12.4 0.1 reshape.82
  12.5 0.6 fusion.54
  13.1 0.1 concatenate.38
  13.2 0.1 broadcast_in_dim.14
  13.2 0.1 add.254
  13.3 0.0 copy-done.14
  13.4 0.1 concatenate.37
  13.5 0.1 concatenate.39
  13.6 0.1 fusion.49
  13.7 0.0 copy-start.4
  13.7 0.8 fusion.18
  14.6 1.4 pad_maximum_fusion.9
  15.9 0.8 concatenate.35
  16.7 0.8 concatenate.40
  17.5 0.1 concatenate.34
  17.6 0.0 copy-start.6
  17.6 0.1 slice.316
  17.7 0.1 slice_reduce_fusion.2
  17.8 2.8 %fusion.13 = f32[512,1024]{1,0:T(8,128)} fusion(f32[1024]{0:T(1024)S(1)} %slice.316, f32[512]{0:T(512)S(1)} %add.254, f32[1024]{0:T(1024)S(1)} %bitcast.73, f32[512]{0:T(512)S(1)} %bitcast.71, f32[1024]{0:T(1024)S(1)} %bitcast.74, f32[512]{0:T(512)S(1)} %bitcast.69, f32[1024]{0:T(1024)S(1)} %bitcast.72, f32[512]{0:T(512)S(1)} %bitcast.67), kind=kLoop, calls=%fused_computation.28 | loop fusion | flops 11534336 | bytes 2121728 | tf_op jit(solution)/shard_map/mul | solution.py:90
  20.6 4.5 %fusion.1 = f32[512,1536]{1,0:T(8,128)} fusion(f32[1536]{0:T(1024)S(1)} %concatenate.35, f32[512]{0:T(512)S(1)} %add.254, f32[1536]{0:T(1024)S(1)} %get-tuple-element.24, f32[512]{0:T(512)} %bitcast.83, f32[1536]{0:T(1024)S(1)} %get-tuple-element.25, f32[512]{0:T(512)S(1)} %bitcast.82, f32[1536]{0:T(1024)S(1)} %get-tuple-element.23, f32[512]{0:T(512)S(1)} %bitcast.81), kind=kLoop, calls=%fused_computation.7 | loop fusion | flops 17301504 | bytes 3178496 | tf_op jit(solution)/shard_map/mul | solution.py:90
  25.1 0.0 copy-done.6
  25.1 1.1 fusion.26
  26.2 5.1 %all-to-all-done = f32[16,96,256]{2,1,0:T(8,128)S(1)} async-done(((f32[16,96,256]{2,1,0:T(8,128)}), f32[16,96,256]{2,1,0:T(8,128)S(1)}, u32[]{:S(2)}, u32[]{:S(2)}) %all-to-all-start) | async-done | bytes 1572896 | tf_op jit(solution)/shard_map/all_to_all | solution.py:30
  31.4 0.6 fusion.22
  32.0 1.0 copy-done.3
  33.0 1.8 %convolution_add_fusion.1 = f32[512,256]{1,0:T(8,128)} fusion(f32[512,256]{1,0:T(8,128)S(1)} %fusion.22, f32[512,1024]{1,0:T(8,128)S(1)} %copy-done.3, f32[1536,256]{1,0:T(8,128)S(1)} %bitcast.57), kind=kOutput, calls=%fused_computation.35 | convolution fusion | flops 805437440 | bytes 4194304 | tf_op jit(solution)/shard_map/dot_general | solution.py:108
  34.8 3.8 %collective-permute-start = (f32[512,256]{1,0:T(8,128)}, f32[512,256]{1,0:T(8,128)S(1)}, u32[]{:S(2)}, u32[]{:S(2)}) collective-permute-start(f32[512,256]{1,0:T(8,128)} %convolution_add_fusion.1), channel_id=1, source_target_pairs={{0,16},{16,0},{1,17},{17,1},{2,18},{18,2},{3,19},{19,3},{4,20},{20... | collective-permute-start | bytes 1572872 | tf_op jit(solution)/shard_map/ppermute | solution.py:39
  38.6 0.4 fusion.28
  39.0 0.9 dynamic-slice_multiply_fusion
  40.0 3.3 %fusion.57 = f32[512,256]{1,0:T(8,128)S(1)} fusion(f32[512,1536]{1,0:T(8,128)} %fusion.1, f32[1536,256]{1,0:T(8,128)S(1)} %bitcast.58), kind=kOutput, calls=%fused_computation.104 | convolution fusion | flops 1207959552 | bytes 5242880 | tf_op jit(solution)/shard_map/dot_general | solution.py:110
  43.3 0.0 collective-permute-done
  43.3 0.9 add.297
  44.2 4.7 %all-to-all-start.1 = ((f32[4,128,256]{2,1,0:T(8,128)}), f32[4,128,256]{2,1,0:T(8,128)S(1)}, u32[]{:S(2)}, u32[]{:S(2)}) async-start(f32[4,128,256]{2,1,0:T(8,128)} %bitcast.14), calls=%async_computation.1 | async-start | bytes 1048576 | tf_op jit(solution)/shard_map/all_to_all | solution.py:30
  48.9 0.0 copy-start.9
  48.9 6.6 %fusion.5 = (f32[1536,512]{1,0:T(8,128)}, f32[1536,512]{1,0:T(8,128)}) fusion(f32[512]{0:T(512)S(1)} %bitcast.76, f32[512]{0:T(512)S(1)} %bitcast.77, f32[512]{0:T(512)S(1)} %bitcast.75, f32[1536]{0:T(1024)S(1)} %concatenate.35, f32[512]{0:T(512)S(1)} %add.254, f32[1536]{0:T(1024)S(1)} %get-tuple-element.24, f32[1536]{0:T(1024)S(1)} %get-tuple-element.25, ...), kind=kLoop, calls=%fused_computation.11 | loop fusion | flops 34603008 | bytes 6330368 | tf_op jit(solution)/shard_map/mul | solution.py:86
  55.5 5.8 %all-to-all-done.1 = f32[4,128,256]{2,1,0:T(8,128)S(1)} async-done(((f32[4,128,256]{2,1,0:T(8,128)}), f32[4,128,256]{2,1,0:T(8,128)S(1)}, u32[]{:S(2)}, u32[]{:S(2)}) %all-to-all-start.1) | async-done | bytes 524320 | tf_op jit(solution)/shard_map/all_to_all | solution.py:30
  61.4 29.2 %all-gather = f32[512,256]{1,0:T(8,128)S(1)} all-gather(f32[128,256]{1,0:T(8,128)S(1)} %reduce_sum.36), channel_id=2, replica_groups=mesh['far'=4,'near'=4,'core'=2,'kvec'=16] {'far'}, dimensions={0}, use_global_device_ids=true | all-gather | bytes 655360 | tf_op jit(solution)/shard_map/all_gather | solution.py:114
  90.7 0.2 fusion.24
  91.0 0.2 fusion.58
  91.2 0.2 convolution_add_fusion.2
  91.5 17.3 %all_gather.11 = f32[512,256]{1,0:T(8,128)S(1)} all-gather(f32[128,256]{1,0:T(8,128)S(1)} %convolution_add_fusion.2), channel_id=1, replica_groups=mesh['far'=4,'near'=4,'core'=2,'kvec'=16] {'near'}, dimensions={0}, use_global_device_ids=true | all-gather | bytes 655360 | tf_op jit(solution)/shard_map/all_gather | solution.py:126
  108.8 6.1 %collective-permute-start.1 = (f32[512,256]{1,0:T(8,128)S(1)}, f32[512,256]{1,0:T(8,128)S(1)}, u32[]{:S(2)}, u32[]{:S(2)}) collective-permute-start(f32[512,256]{1,0:T(8,128)S(1)} %all_gather.11), channel_id=1, source_target_pairs={{0,16},{16,0},{1,17},{17,1},{2,18},{18,2},{3,19},{19,3},{4,20},{20... | collective-permute-start | bytes 1572872 | tf_op jit(solution)/shard_map/ppermute | solution.py:39
  114.9 1.5 fusion.59
  116.3 0.0 collective-permute-done.1
  116.4 2.6 %convolution_add_fusion = f32[1536,256]{1,0:T(8,128)} fusion(f32[1536,256]{1,0:T(8,128)S(1)} %fusion.59, f32[1536,512]{1,0:T(8,128)S(1)} %copy-done.2, f32[512,256]{1,0:T(8,128)S(1)} %collective-permute-done.1), kind=kOutput, calls=%fused_computation.26 | convolution fusion | flops 1208352768 | bytes 6815744 | tf_op jit(solution)/shard_map/dot_general | solution.py:128
  119.0 6.0 %all-to-all-start.2 = ((f32[16,96,256]{2,1,0:T(8,128)}), f32[16,96,256]{2,1,0:T(8,128)S(1)}, u32[]{:S(2)}, u32[]{:S(2)}) async-start(f32[16,96,256]{2,1,0:T(8,128)} %bitcast.59), calls=%async_computation.2 | async-start | bytes 3145728 | tf_op jit(solution)/shard_map/all_to_all | solution.py:30
  125.0 0.5 compare_convert_fusion
  125.6 20.6 %all-to-all-done.2 = f32[16,96,256]{2,1,0:T(8,128)S(1)} async-done(((f32[16,96,256]{2,1,0:T(8,128)}), f32[16,96,256]{2,1,0:T(8,128)S(1)}, u32[]{:S(2)}, u32[]{:S(2)}) %all-to-all-start.2) | async-done | bytes 1572896 | tf_op jit(solution)/shard_map/all_to_all | solution.py:30
  146.2 0.1 reduce_sum.38
  146.3 0.1 multiply_reduce_fusion
  146.4 0.3 fusion.38
  146.7 0.9 fusion.16
  (55 shorter events, 0.3 us)
Async XLA Ops:
  0.0 146.4 %copy-start = (f32[256,512]{1,0:T(8,128)S(1)}, f32[256,512]{1,0:T(8,128)}, u32[]{:S(2)}) copy-start(f32[256,512]{1,0:T(8,128)} %param.21) | copy-start | bytes 1572868
  0.0 13.2 %copy-start.19 = (f32[2]{0:T(128)S(1)}, f32[2]{0:T(128)}, u32[]{:S(2)}) copy-start(f32[2]{0:T(128)} %constant.18.clone) | copy-start | bytes 28
  0.0 9.9 %copy-start.21 = (s32[32]{0:T(128)S(1)}, s32[32]{0:T(128)}, u32[]{:S(2)}) copy-start(s32[32]{0:T(128)} %param.15) | copy-start | bytes 388
  0.0 11.8 %copy-start.10 = (s32[3,1536]{1,0:T(4,128)S(1)}, s32[3,1536]{1,0:T(4,128)}, u32[]{:S(2)}) copy-start(s32[3,1536]{1,0:T(4,128)} %param.13) | copy-start | bytes 55300
  0.0 12.0 %copy-start.12 = (s32[3,512]{1,0:T(4,128)S(1)}, s32[3,512]{1,0:T(4,128)}, u32[]{:S(2)}) copy-start(s32[3,512]{1,0:T(4,128)} %param.14) | copy-start | bytes 18436
  2.3 29.1 %all-to-all-start = ((f32[16,96,256]{2,1,0:T(8,128)}), f32[16,96,256]{2,1,0:T(8,128)S(1)}, u32[]{:S(2)}, u32[]{:S(2)}) async-start(f32[16,96,256]{2,1,0:T(8,128)} %broadcast_in_dim.17), calls=%async_computation | async-start | bytes 3145728 | tf_op jit(solution)/shard_map/all_to_all | solution.py:30
  11.8 1.3 copy-start.11
  11.8 1.6 %copy-start.13 = (f32[96]{0:T(128)}, f32[96]{0:T(128)S(1)}, u32[]{:S(2)}) copy-start(f32[96]{0:T(128)S(1)} %get-tuple-element.79) | copy-start | bytes 1156
  11.8 1.6 %copy-start.14 = (f32[96]{0:T(128)}, f32[96]{0:T(128)S(1)}, u32[]{:S(2)}) copy-start(f32[96]{0:T(128)S(1)} %get-tuple-element.80) | copy-start | bytes 1156
  11.8 1.6 %copy-start.15 = (f32[96]{0:T(128)}, f32[96]{0:T(128)S(1)}, u32[]{:S(2)}) copy-start(f32[96]{0:T(128)S(1)} %get-tuple-element.81) | copy-start | bytes 1156
  11.8 1.9 %copy-start.16 = (f32[96]{0:T(128)}, f32[96]{0:T(128)S(1)}, u32[]{:S(2)}) copy-start(f32[96]{0:T(128)S(1)} %get-tuple-element.82) | copy-start | bytes 1156
  11.8 1.9 %copy-start.17 = (f32[96]{0:T(128)}, f32[96]{0:T(128)S(1)}, u32[]{:S(2)}) copy-start(f32[96]{0:T(128)S(1)} %get-tuple-element.83) | copy-start | bytes 1156
  13.7 11.4 %copy-start.4 = (f32[256,256]{1,0:T(8,128)S(1)}, f32[256,256]{1,0:T(8,128)}, u32[]{:S(2)}) copy-start(f32[256,256]{1,0:T(8,128)} %param.19) | copy-start | bytes 786436
  17.6 7.5 %copy-start.6 = (f32[2,256,256]{2,1,0:T(8,128)S(1)}, f32[2,256,256]{2,1,0:T(8,128)}, u32[]{:S(2)}) copy-start(f32[2,256,256]{2,1,0:T(8,128)} %param.18) | copy-start | bytes 1572868
  31.4 1.6 %copy-start.3 = (f32[512,1024]{1,0:T(8,128)S(1)}, f32[512,1024]{1,0:T(8,128)}, u32[]{:S(2)}) copy-start(f32[512,1024]{1,0:T(8,128)} %fusion.13) | copy-start | bytes 6291460
  31.4 7.3 %copy-start.7 = (f32[2,256,256]{2,1,0:T(8,128)S(1)}, f32[2,256,256]{2,1,0:T(8,128)}, u32[]{:S(2)}) copy-start(f32[2,256,256]{2,1,0:T(8,128)} %param.18) | copy-start | bytes 1572868
  34.8 8.5 %collective-permute-start = (f32[512,256]{1,0:T(8,128)}, f32[512,256]{1,0:T(8,128)S(1)}, u32[]{:S(2)}, u32[]{:S(2)}) collective-permute-start(f32[512,256]{1,0:T(8,128)} %convolution_add_fusion.1), channel_id=1, source_target_pairs={{0,16},{16,0},{1,17},{17,1},{2,18},{18,2},{3,19},{19,3},{4,20},{20... | collective-permute-start | bytes 1572872 | tf_op jit(solution)/shard_map/ppermute | solution.py:39
  44.2 17.2 %all-to-all-start.1 = ((f32[4,128,256]{2,1,0:T(8,128)}), f32[4,128,256]{2,1,0:T(8,128)S(1)}, u32[]{:S(2)}, u32[]{:S(2)}) async-start(f32[4,128,256]{2,1,0:T(8,128)} %bitcast.14), calls=%async_computation.1 | async-start | bytes 1048576 | tf_op jit(solution)/shard_map/all_to_all | solution.py:30
  48.9 41.7 %copy-start.9 = (f32[256,256]{1,0:T(8,128)S(1)}, f32[256,256]{1,0:T(8,128)}, u32[]{:S(2)}) copy-start(f32[256,256]{1,0:T(8,128)} %param.16) | copy-start | bytes 786436
  55.5 35.7 %copy-start.5 = (f32[256,256]{1,0:T(8,128)S(1)}, f32[256,256]{1,0:T(8,128)}, u32[]{:S(2)}) copy-start(f32[256,256]{1,0:T(8,128)} %fusion.26) | copy-start | bytes 786436
  90.6 24.2 %copy-start.1 = (f32[1536,512]{1,0:T(8,128)S(1)}, f32[1536,512]{1,0:T(8,128)}, u32[]{:S(2)}) copy-start(f32[1536,512]{1,0:T(8,128)} %get-tuple-element.20) | copy-start | bytes 9437188
  91.2 25.2 %copy-start.2 = (f32[1536,512]{1,0:T(8,128)S(1)}, f32[1536,512]{1,0:T(8,128)}, u32[]{:S(2)}) copy-start(f32[1536,512]{1,0:T(8,128)} %get-tuple-element.22) | copy-start | bytes 9437188
  108.8 7.6 %collective-permute-start.1 = (f32[512,256]{1,0:T(8,128)S(1)}, f32[512,256]{1,0:T(8,128)S(1)}, u32[]{:S(2)}, u32[]{:S(2)}) collective-permute-start(f32[512,256]{1,0:T(8,128)S(1)} %all_gather.11), channel_id=1, source_target_pairs={{0,16},{16,0},{1,17},{17,1},{2,18},{18,2},{3,19},{19,3},{4,20},{20... | collective-permute-start | bytes 1572872 | tf_op jit(solution)/shard_map/ppermute | solution.py:39
  119.0 27.3 %copy-start.8 = (f32[96,256]{1,0:T(8,128)S(1)}, f32[96,256]{1,0:T(8,128)}, u32[]{:S(2)}) copy-start(f32[96,256]{1,0:T(8,128)} %param.12) | copy-start | bytes 294916
  119.0 27.4 %copy-start.18 = (f32[256]{0:T(256)S(1)}, f32[256]{0:T(256)}, u32[]{:S(2)}) copy-start(f32[256]{0:T(256)} %param.20) | copy-start | bytes 3076
  119.0 27.7 %copy-start.20 = (f32[512,256]{1,0:T(8,128)S(1)}, f32[512,256]{1,0:T(8,128)}, u32[]{:S(2)}) copy-start(f32[512,256]{1,0:T(8,128)} %param.22) | copy-start | bytes 1572868
  119.0 27.2 %all-to-all-start.2 = ((f32[16,96,256]{2,1,0:T(8,128)}), f32[16,96,256]{2,1,0:T(8,128)S(1)}, u32[]{:S(2)}, u32[]{:S(2)}) async-start(f32[16,96,256]{2,1,0:T(8,128)} %bitcast.59), calls=%async_computation.2 | async-start | bytes 3145728 | tf_op jit(solution)/shard_map/all_to_all | solution.py:30
